TPU v7x, 128 devices: a whole 4x4x4 slice. The times are simulated.
128 devices in a mesh: row: 8 (over x, core), col: 16 (over y, z).
Axes of the slice: x: 4, y: 4, z: 4, core: 2. Of those that a mesh axis runs over, the one named last changes fastest.
Arguments:
- image_pooled: bfloat16 [16384, 1664], P(('row', 'col')), may hold values from -6 to 6
- text_pooled: bfloat16 [16384, 1280], P(('col', 'row')), may hold values from -6 to 6
- image_proj: bfloat16 [1664, 1280], replicated, may hold values from -0.8 to 0.8
- text_proj: bfloat16 [1280, 1280], replicated, may hold values from -0.8 to 0.8
- log_scale: float32 [1], replicated, may hold values from 3 to 5.1
- pair_index: int32 [16384], P(('row', 'col')), may hold values from 0 to 16383, each once
Outputs:
- loss: float32 [1], replicated
- d_image_pooled: bfloat16 [16384, 1664], P(('row', 'col'))
- d_text_pooled: bfloat16 [16384, 1280], P(('col', 'row'))
- d_image_proj: float32 [1664, 1280], replicated
- d_text_proj: float32 [1280, 1280], replicated
- d_log_scale: float32 [1], replicated
Inputs may be any that keep to these rules, and one draw needn't show every extreme that they name: `pair_index`: a permutation: every text matches exactly one image.
All inputs are finite; a program needn't handle non-finite values.
Results may differ from a plain program's by a relative error of at most 0.033.
Values may be sent and summed in bfloat16 or wider, within the bound.
A program may use at most 128 MiB of HBM per device.

v0:
```python
import jax
import jax.numpy as jnp
from jax import lax
from jax.sharding import PartitionSpec as P

EPS = 1e-06


def embed(pooled, proj):
    z = jnp.dot(pooled, proj, preferred_element_type=jnp.float32)
    norms = jnp.sqrt(jnp.sum(z * z, axis=1, keepdims=True) + EPS)
    unit = z / norms
    return (unit, norms, unit.astype(jnp.bfloat16))


def normal_grad(grads, unit, norms, proj):
    inner = jnp.sum(unit * grads, axis=1, keepdims=True)
    dz = ((grads - unit * inner) / norms).astype(jnp.bfloat16)
    dpool = lax.dot_general(
        dz, proj, (((1,), (1,)), ((), ())), preferred_element_type=jnp.float32
    ).astype(jnp.bfloat16)
    return (dz, dpool)


def weight_term(pooled, dz):
    return lax.dot_general(pooled, dz, (((0,), (0,)), ((), ())), preferred_element_type=jnp.float32)


def local(image_pooled, text_pooled, image_proj, text_proj, log_scale, pair_index):
    unit_img, norm_img, emb_img = embed(image_pooled, image_proj)
    unit_txt, norm_txt, emb_txt = embed(text_pooled, text_proj)
    scale = jnp.exp(log_scale[0])
    img_block, perm_block = (
        lax.all_gather(emb_img, "col", axis=0, tiled=True),
        lax.all_gather(pair_index, "col", axis=0, tiled=True),
    )
    txt_block = lax.all_gather(emb_txt, "row", axis=0, tiled=True)
    scores = scale * lax.dot_general(
        img_block, txt_block, (((1,), (1,)), ((), ())), preferred_element_type=jnp.float32
    )
    col_width = txt_block.shape[0]
    col_start = lax.axis_index("col") * col_width
    hits = perm_block[:, None] == col_start + lax.iota(jnp.int32, col_width)[None, :]
    row_peak = jnp.max(scores, axis=1)
    col_peak = jnp.max(scores, axis=0)
    row_peak = lax.pmax(row_peak, "col")
    col_peak = lax.pmax(col_peak, "row")
    row_total = lax.psum(jnp.sum(jnp.exp(scores - row_peak[:, None]), axis=1), "col")
    col_total = lax.psum(jnp.sum(jnp.exp(scores - col_peak[None, :]), axis=0), "row")
    lse_row = row_peak + jnp.log(row_total)
    lse_col = col_peak + jnp.log(col_total)
    grad = 0.5 * (
        jnp.exp(scores - lse_row[:, None]) + jnp.exp(scores - lse_col[None, :])
    ) - hits.astype(jnp.float32)
    grad_b = grad.astype(jnp.bfloat16)
    own_img = image_pooled.shape[0]
    own_txt = text_pooled.shape[0]
    row_slice = lax.dynamic_slice_in_dim(lse_row, lax.axis_index("col") * own_img, own_img)
    col_slice = lax.dynamic_slice_in_dim(lse_col, lax.axis_index("row") * own_txt, own_txt)
    part_loss = 0.5 * (jnp.sum(row_slice) + jnp.sum(col_slice)) - jnp.sum(
        jnp.where(hits, scores, 0.0)
    )
    part_scale = jnp.sum(grad * scores)
    stacked = jnp.stack([part_loss, part_scale])
    piece = grad_b
    img_grads = lax.psum_scatter(
        (scale * jnp.dot(piece, txt_block, preferred_element_type=jnp.float32)).astype(
            jnp.bfloat16
        ),
        "col",
        scatter_dimension=0,
        tiled=True,
    ).astype(jnp.float32)
    piece = grad_b
    txt_grads = lax.psum_scatter(
        (
            scale
            * lax.dot_general(
                piece, img_block, (((0,), (0,)), ((), ())), preferred_element_type=jnp.float32
            )
        ).astype(jnp.bfloat16),
        "row",
        scatter_dimension=0,
        tiled=True,
    ).astype(jnp.float32)
    dz_img, dpi = normal_grad(img_grads, unit_img, norm_img, image_proj)
    dz_txt, dpt = normal_grad(txt_grads, unit_txt, norm_txt, text_proj)
    dwi, dwt, totals = lax.psum(
        (weight_term(image_pooled, dz_img), weight_term(text_pooled, dz_txt), stacked),
        ("row", "col"),
    )
    batch_rows = own_img * lax.axis_size("row") * lax.axis_size("col")
    loss = (totals[0] / batch_rows).reshape(1)
    return (loss, dpi, dpt, dwi, dwt, totals[1].reshape(1))


def solution(mesh):
    return jax.shard_map(
        local,
        mesh=mesh,
        in_specs=(
            P(("row", "col"), None),
            P(("col", "row"), None),
            P(),
            P(),
            P(),
            P(("row", "col")),
        ),
        out_specs=(P(), P(("row", "col"), None), P(("col", "row"), None), P(), P(), P()),
        check_vma=False,
    )
```

profile of v0, /device:TPU:1, one launch (start us, length us, event | category | flops | bytes accessed | tf_op | source)
XLA Modules:
  0.0 559.8 jit_solution(14864642687246588171)
XLA Ops:
  7.2 0.0 copy-start
  7.2 0.0 all-gather.6.cloned.1.call-start
  7.2 1.9 copy-done
  9.1 1.7 multiply_reduce_fusion.3
  10.8 0.8 copy-done.1
  11.6 0.8 fusion.10
  12.5 0.0 all-gather.6.cloned.1.call-update
  12.5 0.0 all-gather.4.cloned.1.call-start
  12.5 3.2 multiply_reduce_fusion.4
  15.8 0.8 copy-done.2
  16.6 0.8 fusion.9
  17.4 0.0 all-gather.4.cloned.1.call-update
  17.5 0.0 reduce-scatter.5.cloned.1.call-start
  18.2 19.7 %all-gather = s32[16,1,128]{2,1,0:T(1,128)S(1)} all-gather(s32[1,1,128]{2,1,0:T(1,128)S(1)} %bitcast.24), channel_id=1, replica_groups=mesh['row'=8,'col'=16] {'col'}, dimensions={0}, use_global_device_ids=true | all-gather | bytes 8704 | tf_op jit(solution)/shard_map/all_gather | solution.py:35
  37.9 4.4 all-gather.6.cloned.1.call-done
  42.4 59.4 %all-gather.4.cloned.1.call-done = bf16[2048,1280]{1,0:T(8,128)(2,1)} async-done(((bf16[128,1280]{1,0:T(8,128)(2,1)}), bf16[2048,1280]{1,0:T(8,128)(2,1)}) %all-gather.4.cloned.1.call-update) | async-done | bytes 5242896 | tf_op jit(solution)/shard_map/all_gather | solution.py:34
  101.8 10.9 %multiply_reduce_fusion.2 = (f32[2048]{0:T(1024)S(1)}, f32[2048,1024]{1,0:T(8,128)}) fusion(f32[]{:T(128)} %bitcast, bf16[2048,1280]{1,0:T(8,128)(2,1)} %all-gather.4.cloned.1.call-done, bf16[1024,1280]{1,0:T(8,128)(2,1)} %all-gather.6.cloned.1.call-done), kind=kOutput, calls=%fused_computation.12 | convolution fusion | flops 5372901376 | bytes 16261124 | tf_op jit(solution)/shard_map/dot_general | solution.py:38
  112.6 32.0 %pmax.14 = f32[2048]{0:T(1024)S(1)} all-reduce(f32[2048]{0:T(1024)S(1)} %get-tuple-element.31), channel_id=1, replica_groups=mesh['row'=8,'col'=16] {'col'}, use_global_device_ids=true, to_apply=%region_3.0 | all-reduce | flops 2048 | bytes 16384 | tf_op jit(solution)/shard_map/pmax | solution.py:46
  144.7 4.5 exponential_reduce_fusion.1
  149.1 29.0 %psum.35 = f32[2048]{0:T(1024)S(1)} all-reduce(f32[2048]{0:T(1024)S(1)} %get-tuple-element.20), channel_id=1, replica_groups=mesh['row'=8,'col'=16] {'col'}, use_global_device_ids=true, to_apply=%region_5.0 | all-reduce | flops 2048 | bytes 16384 | tf_op jit(solution)/shard_map/psum | solution.py:48
  178.2 26.3 %pmax.15 = f32[1024]{0:T(1024)S(1)} all-reduce(f32[1024]{0:T(1024)S(1)} %get-tuple-element.21), channel_id=1, replica_groups=mesh['row'=8,'col'=16] {'row'}, use_global_device_ids=true, to_apply=%region_8.0 | all-reduce | flops 1024 | bytes 8192 | tf_op jit(solution)/shard_map/pmax | solution.py:47
  204.5 4.8 exponential_reduce_fusion
  209.3 12.6 %psum.36 = f32[1024]{0:T(1024)S(1)} all-reduce(f32[1024]{0:T(1024)S(1)} %exponential_reduce_fusion), channel_id=1, replica_groups=mesh['row'=8,'col'=16] {'row'}, use_global_device_ids=true, to_apply=%region_10.0 | all-reduce | flops 1024 | bytes 8192 | tf_op jit(solution)/shard_map/psum | solution.py:49
  221.9 9.2 %fusion = (f32[]{:T(128)}, f32[]{:T(128)}, bf16[2048,1024]{1,0:T(8,128)(2,1)S(1)}) fusion(f32[2048,1024]{1,0:T(8,128)} %get-tuple-element.32, s32[1024]{0:T(1024)S(1)} %iota_add_fusion, f32[]{:T(128)} %bitcast, s32[2048]{0:T(1024)S(1)} %bitcast.23, f32[1024]{0:T(1024)S(1)} %log_add_fusion.1, f32[2048]{0:T(1024)S(1)} %log_add_fusion), kind=kLoop, calls=%fused_computation.5 | loop fusion | flops 27262976 | bytes 12607500 | tf_op jit(solution)/shard_map/reduce_sum | solution.py:60
  231.1 2.0 copy-done.4
  233.1 7.1 %multiply_convert_fusion.1 = bf16[1024,1280]{1,0:T(8,128)(2,1)} fusion(bf16[2048,1024]{1,0:T(8,128)(2,1)S(1)} %get-tuple-element.24, bf16[2048,1280]{1,0:T(8,128)(2,1)S(1)} %bitcast.26, f32[]{:T(128)} %bitcast), kind=kOutput, calls=%fused_computation.13 | convolution fusion | flops 5371330560 | bytes 12058628 | tf_op jit(solution)/shard_map/dot_general | solution.py:78
  240.2 0.0 reduce-scatter.5.cloned.1.call-update
  240.2 0.0 reduce-scatter.3.cloned.1.call-start
  240.3 9.6 %multiply_convert_fusion = bf16[2048,1280]{1,0:T(8,128)(2,1)} fusion(bf16[2048,1024]{1,0:T(8,128)(2,1)} %copy-done.4, bf16[1024,1280]{1,0:T(8,128)(2,1)} %all-gather.6.cloned.1.call-done, f32[]{:T(128)} %bitcast), kind=kOutput, calls=%fused_computation.2 | convolution fusion | flops 5373952000 | bytes 12058628 | tf_op jit(solution)/shard_map/dot_general | solution.py:67
  249.9 0.0 reduce-scatter.3.cloned.1.call-update
  250.0 0.0 all-reduce.3.cloned.1.call-start
  250.0 17.3 %reduce-scatter.5.cloned.1.call-done = bf16[128,1280]{1,0:T(8,128)(2,1)} async-done(((bf16[1024,1280]{1,0:T(8,128)(2,1)}), bf16[128,1280]{1,0:T(8,128)(2,1)}) %reduce-scatter.5.cloned.1.call-update) | async-done | bytes 327696 | tf_op jit(solution)/shard_map/reduce_scatter | solution.py:75
  267.4 1.4 fusion.6
  268.8 5.2 convolution_bitcast_fusion
  274.0 77.1 %reduce-scatter.3.cloned.1.call-done = bf16[128,1280]{1,0:T(8,128)(2,1)} async-done(((bf16[2048,1280]{1,0:T(8,128)(2,1)}), bf16[128,1280]{1,0:T(8,128)(2,1)}) %reduce-scatter.3.cloned.1.call-update) | async-done | bytes 327696 | tf_op jit(solution)/shard_map/reduce_scatter | solution.py:66
  351.1 1.4 fusion.3
  352.6 6.2 %convolution_bitcast_fusion.1 = f32[1664,1280]{0,1:T(8,128)} fusion(bf16[128,1664]{1,0:T(8,128)(2,1)} %param.6, bf16[128,1280]{1,0:T(8,128)(2,1)} %reduce-scatter.3.cloned.1.call-done, f32[128]{0:T(128)S(1)} %fusion.3, f32[128]{0:T(128)S(1)} %add_sqrt_fusion.1, f32[128,1280]{1,0:T(8,128)} %copy-done.2), kind=kOutput, calls=%fused_computation.4 | convolution fusion | flops 546242560 | bytes 9929728 | tf_op jit(solution)/shard_map/dot_general | solution.py:26
  358.7 0.0 all-reduce.3.cloned.1.call-update
  358.8 0.7 dynamic-slice_reduce_fusion.1
  359.4 0.7 dynamic-slice_reduce_fusion
  362.1 0.7 pad_maximum_fusion
  362.8 66.4 %psum.37 = f32[2]{0:T(128)S(1)} all-reduce(f32[2]{0:T(128)S(1)} %pad_maximum_fusion), channel_id=1, replica_groups=mesh['row'=8,'col'=16] {'row','col'}, use_global_device_ids=true, to_apply=%region_14.15 | all-reduce | flops 2 | bytes 16 | tf_op jit(solution)/shard_map/psum | solution.py:88
  429.1 0.6 fusion.15
  430.4 3.1 convolution_convert_fusion.1
  433.5 4.5 convolution_convert_fusion
  438.0 96.1 %all-reduce.3.cloned.1.call-done = (f32[1664,1280]{0,1:T(8,128)}, f32[1280,1280]{0,1:T(8,128)}) async-done(((f32[1664,1280]{0,1:T(8,128)}, f32[1280,1280]{0,1:T(8,128)}), (f32[1664,1280]{0,1:T(8,128)}, f32[1280,1280]{0,1:T(8,128)})) %all-reduce.3.cloned.1.call-update) | async-done | bytes 15073296 | tf_op jit(solution)/shard_map/psum | solution.py:88
  534.1 9.9 %copy.14 = f32[1664,1280]{1,0:T(8,128)} copy(f32[1664,1280]{0,1:T(8,128)} %get-tuple-element.22) | data formatting | bytes 17039360
  544.0 8.1 %copy.15 = f32[1280,1280]{1,0:T(8,128)} copy(f32[1280,1280]{0,1:T(8,128)} %get-tuple-element.23) | data formatting | bytes 13107200
  (19 shorter events, 0.1 us)
Async XLA Ops:
  7.2 1.9 copy-start
  7.2 11.0 %copy-start.6 = (s32[128]{0:T(128)S(1)}, s32[128]{0:T(128)}, u32[]{:S(2)}) copy-start(s32[128]{0:T(128)} %param.11) | copy-start | bytes 1540
  7.2 35.2 %all-gather.6.cloned.1.call-start = ((), (), s32[]{:S(2)}) async-start(), calls=%async_computation.3 | async-start | bytes 2949120 | tf_op jit(solution)/shard_map/all_gather | solution.py:37
  10.8 0.8 copy-start.1
  12.5 89.3 %all-gather.4.cloned.1.call-start = ((), (), s32[]{:S(2)}) async-start(), calls=%async_computation.2 | async-start | bytes 5570560 | tf_op jit(solution)/shard_map/all_gather | solution.py:34
  15.7 0.9 copy-start.2
  17.5 249.9 %reduce-scatter.5.cloned.1.call-start = ((), (), s32[]{:S(2)}) async-start(), calls=%async_computation.5 | async-start | bytes 2949120 | tf_op jit(solution)/shard_map/reduce_scatter | solution.py:75
  221.9 11.2 %slice-start = ((s8[5242880]{0:T(1024)(128)(4,1)}), s8[4194304]{0:T(1024)(128)(4,1)S(1)}, s32[]{:S(2)}) async-start(s8[5242880]{0:T(1024)(128)(4,1)} %bitcast.25), calls=%async_computation.7 | async-start | bytes 8388608
  221.9 11.2 %slice-start.1 = ((s8[5242880]{0:T(1024)(128)(4,1)}), s8[1048576]{0:T(1024)(128)(4,1)S(1)}, s32[]{:S(2)}) async-start(s8[5242880]{0:T(1024)(128)(4,1)} %bitcast.25), calls=%async_computation.8 | async-start | bytes 2097152
  231.1 2.0 copy-start.4
  240.2 110.9 %reduce-scatter.3.cloned.1.call-start = ((), (), s32[]{:S(2)}) async-start(), calls=%async_computation.4 | async-start | bytes 5570560 | tf_op jit(solution)/shard_map/reduce_scatter | solution.py:66
  250.0 284.1 %all-reduce.3.cloned.1.call-start = ((), (), s32[]{:S(2)}) async-start(), calls=%async_computation.6 | async-start | bytes 30146560 | tf_op jit(solution)/shard_map/psum | solution.py:88
  429.1 4.4 copy-start.3
  429.1 4.4 copy-start.5
Sparse Core Ops, SparseCore 0:
  12.6 29.7 all-gather.5
  45.1 56.6 all-gather.3
  240.4 26.9 reduce-scatter.4
  271.1 79.9 reduce-scatter.2
  358.9 175.1 all-reduce.2
where the time goes:
time: 561 us; the launch traced here: 560 us
  waiting for transfers between devices  254 us (45%)
  blocking collectives  186 us (33%)
  matrix products  51.5 us (9%)
  other arithmetic  25.1 us (4%)
  local copies, waits for them, and re-layouts  24.2 us (4%)
  between operations  18.3 us (3%)
    psum x1, waiting for transfers between devices, local(): lax.psum((weight_term(image_pooled, dz_img), weight_term(text_pooled, dz_...  96.1 us
    reduce_scatter x1, waiting for transfers between devices, local(): lax.psum_scatter((scale * jnp.dot(piece, txt_block, preferred_element_typ...  77.1 us
    psum x1, blocking collectives, local(): lax.psum((weight_term(image_pooled, dz_img), weight_term(text_pooled, dz_...  66.4 us
    all_gather x1, waiting for transfers between devices, local(): lax.all_gather(emb_img, 'col', axis=0, tiled=True)  59.4 us
    pmax x1, blocking collectives, local(): row_peak = lax.pmax(row_peak, 'col')  32 us
    psum x1, blocking collectives, local(): lax.psum(jnp.sum(jnp.exp(scores - row_peak[:, None]), axis=1), 'col')  29 us
    pmax x1, blocking collectives, local(): col_peak = lax.pmax(col_peak, 'row')  26.3 us
    unnamed x20, local copies, waits for them, and re-layouts  23.6 us
  transfers between devices with their start and end apart: 5, of which 5 were waited for; matrix products, arithmetic and copies ran while one was open for 5% of the time, Pallas kernels for 0%

commit v1 on v0

v1 whole, which is shorter than its diff:
```python
import functools

import jax
import jax.numpy as jnp
from jax import lax
from jax.experimental import pallas as pl
from jax.experimental.pallas import tpu as pltpu
from jax.sharding import PartitionSpec as P

EPS = 1e-06
MESH = pl.DeviceIdType.MESH
F32 = jnp.float32
BF16 = jnp.bfloat16
PAIRS = 128
NCOL = 16
NROW = 8
EMB = 1280
DI = 1664
DT = 1280
HALF = EMB // 2
DIRS = (1, -1)
STEPS = (2, 1, -1, 0)


class Net:
    def __init__(self, send_sem, recv_sem):
        self.send_sem, self.recv_sem = send_sem, recv_sem
        row, col = lax.axis_index("row"), lax.axis_index("col")
        self.x, self.c = row // 2, row % 2
        self.y, self.z = col // 4, col % 4
        self.count = 0
        self.started = []

    def dev(self, dx=0, dy=0, dz=0):
        return (
            2 * ((self.x + dx + 4) % 4) + self.c,
            4 * ((self.y + dy + 4) % 4) + (self.z + dz + 4) % 4,
        )

    def mate(self):
        return (2 * self.x + 1 - self.c, 4 * self.y + self.z)

    def barrier(self):
        others = [self.mate()]
        for d in (1, 2, 3):
            others += [self.dev(dx=d), self.dev(dy=d), self.dev(dz=d)]
        sem = pltpu.get_barrier_semaphore()
        for other in others:
            pl.semaphore_signal(sem, inc=1, device_id=other, device_id_type=MESH)
        pl.semaphore_wait(sem, len(others))

    def copy(self, number, src, dst, device):
        return pltpu.make_async_remote_copy(
            src_ref=src,
            dst_ref=dst,
            send_sem=self.send_sem.at[number],
            recv_sem=self.recv_sem.at[number],
            device_id=device,
            device_id_type=MESH,
        )

    def send(self, src, dst, device):
        number = self.count
        self.count += 1
        copy = self.copy(number, src, dst, device)
        copy.start()
        self.started.append(copy)
        return number

    def recv(self, number, dst):
        self.copy(number, dst, dst, self.mate()).wait_recv()

    def finish(self):
        for copy in self.started:
            copy.wait_send()


def lanes(column):
    return jnp.transpose(jnp.broadcast_to(column, (PAIRS, PAIRS)))[0:1, :]


def sublanes(row):
    return jnp.transpose(jnp.broadcast_to(row, (PAIRS, PAIRS)))


def lse_over(parts):
    peak = functools.reduce(jnp.maximum, parts)
    return peak + jnp.log(sum(jnp.exp(p - peak) for p in parts))


def main_kernel(
    scale_ref, eimg, etxt, pair, gimg, gtxt, sums,
    img, txt, pid, scores, gb, pimg, ptxt,
    rg1, rg2, rb, rf1, rf2, rc, rx1, rx2,
    cmax, csum, rowl, rowz, rowy, coll, colx, colc, acc, send_sem, recv_sem,
):
    net = Net(send_sem, recv_sem)
    x, c, y, z = net.x, net.c, net.y, net.z
    me_col = 4 * y + z
    scale = scale_ref[0]

    def axes(h):
        return ((y, z), (z, y))[h]

    def gdev(h, d):
        return net.dev(dy=d) if h == 0 else net.dev(dz=d)

    def fdev(h, d):
        return net.dev(dz=d) if h == 0 else net.dev(dy=d)

    def block(h, dg, df):
        g, f = axes(h)
        g, f = (g + dg + 4) % 4, (f + df + 4) % 4
        return 4 * g + f if h == 0 else 4 * f + g

    def half(ref, q, h):
        return ref.at[q, pl.ds(64 * h, 64)]

    def sub(ref, q, h, d):
        return ref.at[q, pl.ds(64 * h + (0 if d == 1 else 32), 32)]

    def rel(dy, dz):
        return 4 * ((y + dy + 4) % 4) + (z + dz + 4) % 4

    def tblock(dx, core):
        return pl.ds(pl.multiple_of((2 * ((x + dx + 4) % 4) + core) * PAIRS, PAIRS), PAIRS)

    def tsub(dx, core, d):
        start = (2 * ((x + dx + 4) % 4) + core) * PAIRS + (0 if d == 1 else 64)
        return pl.ds(pl.multiple_of(start, 64), 64)

    img[me_col] = eimg[...]
    txt[tblock(0, c), :] = etxt[...]
    pid[me_col] = jnp.broadcast_to(pair[...], (8, PAIRS))
    cmax[...] = jnp.full_like(cmax, -1e30)
    csum[...] = jnp.zeros_like(csum)
    acc[...] = jnp.zeros_like(acc)
    net.barrier()

    f1, g1, f2, g3, g4 = {}, {}, {}, {}, {}
    for h in (0, 1):
        for d in DIRS:
            part = half(img, me_col, h)
            f1[h, d] = net.send(part, part, fdev(h, d))
    x1, x2, cx = {}, {}, {}
    for d in DIRS:
        part = txt.at[tblock(0, c)]
        x1[d] = net.send(part, part, net.dev(dx=d))
    for h in (0, 1):
        for d in DIRS:
            part = half(img, me_col, h)
            g1[h, d] = net.send(part, part, gdev(h, d))

    def to_mate(dx):
        part = txt.at[tblock(dx, c)]
        cx[dx] = net.send(part, part, net.mate())

    to_mate(0)
    pz, py = {}, {}
    for d in (1, 2, 3):
        pz[d] = net.send(pid.at[me_col], pid.at[me_col], net.dev(dz=d))

    for h in (0, 1):
        for d in DIRS:
            q = block(h, 0, -d)
            net.recv(f1[h, d], half(img, q, h))
            f2[h, d] = net.send(sub(img, q, h, d), sub(img, q, h, d), fdev(h, d))
            for e in DIRS:
                g3[h, -d, e] = net.send(half(img, q, h), half(img, q, h), gdev(h, e))

    def pass_on(h, j, d):
        q = block(h, -d, j)
        net.recv(g1[h, d] if j == 0 else g3[h, j, d], half(img, q, h))
        g4[h, j, d] = net.send(sub(img, q, h, d), sub(img, q, h, d), gdev(h, d))

    for h in (0, 1):
        for d in DIRS:
            pass_on(h, 0, d)
    for d in DIRS:
        net.recv(x1[d], txt.at[tblock(-d, c)])
        part = txt.at[tsub(-d, c, d)]
        x2[d] = net.send(part, part, net.dev(dx=d))
        to_mate(-d)
    for h in (0, 1):
        q = block(h, 0, 2)
        for d in DIRS:
            net.recv(f2[h, d], sub(img, q, h, d))
        for d in DIRS:
            g3[h, 2, d] = net.send(half(img, q, h), half(img, q, h), gdev(h, d))
    for d in (1, 2, 3):
        net.recv(pz[d], pid.at[rel(0, -d)])
    for d in (1, 2, 3):
        line = pid.at[pl.ds(4 * y, 4)]
        py[d] = net.send(line, line, net.dev(dy=d))
    for d in DIRS:
        net.recv(x2[d], txt.at[tsub(2, c, d)])
    to_mate(2)
    for dx in (0, 1, -1, 2):
        net.recv(cx[dx], txt.at[tblock(dx, 1 - c)])

    def score(q):
        s = scale * lax.dot_general(
            img[q], txt[...], (((1,), (1,)), ((), ())), preferred_element_type=F32
        )
        scores[q] = s
        peak = jnp.max(s, axis=1, keepdims=True)
        total = jnp.sum(jnp.exp(s - peak), axis=1, keepdims=True)
        rowl[pl.ds(q, 1), :] = lanes(peak + jnp.log(total))
        s3 = s.reshape(PAIRS // 8, 8, s.shape[1])
        old = cmax[...]
        new = jnp.maximum(old, jnp.max(s3, axis=0))
        csum[...] = csum[...] * jnp.exp(old - new) + jnp.sum(jnp.exp(s3 - new[None]), axis=0)
        cmax[...] = new

    def score_line(start, length, where):
        @pl.loop(start, start + length)
        def _(i):
            score(where(i))

    score_line(-1, 3, lambda i: rel(0, i))
    for h in (0, 1):
        for j in (1, -1):
            for d in DIRS:
                pass_on(h, j, d)
    score_line(-1, 3, lambda i: rel(1, i))
    for h in (0, 1):
        for d in DIRS:
            pass_on(h, 2, d)
    score_line(-1, 3, lambda i: rel(-1, i))
    for j in (0, 1, -1):
        for h in (0, 1):
            for d in DIRS:
                net.recv(g4[h, j, d], sub(img, block(h, 2, j), h, d))
    score_line(-1, 3, lambda i: rel(2, i))
    score_line(-1, 3, lambda i: rel(i, 2))
    for h in (0, 1):
        for d in DIRS:
            net.recv(g4[h, 2, d], sub(img, block(h, 2, 2), h, d))
    score(rel(2, 2))

    rz, ry, lx = {}, {}, {}
    rowz[z] = rowl[...]
    for d in (1, 2, 3):
        rz[d] = net.send(rowz.at[z], rowz.at[z], net.dev(dz=d))
    peak = jnp.max(cmax[...], axis=0, keepdims=True)
    lcol = peak + jnp.log(jnp.sum(csum[...] * jnp.exp(cmax[...] - peak), axis=0, keepdims=True))
    for r in range(NROW):
        coll[r : r + 1, :] = lcol[:, r * PAIRS : (r + 1) * PAIRS]
    colx[x] = coll[...]
    for d in (1, 2, 3):
        lx[d] = net.send(colx.at[x], colx.at[x], net.dev(dx=d))
    for d in (1, 2, 3):
        net.recv(rz[d], rowz.at[(z - d + 4) % 4])
    rowy[y] = lse_over([rowz[i] for i in range(4)])
    for d in (1, 2, 3):
        ry[d] = net.send(rowy.at[y], rowy.at[y], net.dev(dy=d))
    for d in (1, 2, 3):
        net.recv(lx[d], colx.at[(x - d + 4) % 4])
    colc[c] = lse_over([colx[i] for i in range(4)])
    lc = net.send(colc.at[c], colc.at[c], net.mate())
    for d in (1, 2, 3):
        line = pid.at[pl.ds(4 * ((y - d + 4) % 4), 4)]
        net.recv(py[d], line)
    for d in (1, 2, 3):
        net.recv(ry[d], rowy.at[(y - d + 4) % 4])
    rowl[...] = lse_over([rowy[i] for i in range(4)])
    net.recv(lc, colc.at[1 - c])
    coll[...] = lse_over([colc[i] for i in range(2)])

    first = (me_col * NROW * PAIRS).astype(F32)
    place = lax.broadcasted_iota(jnp.int32, (PAIRS, PAIRS), 1).astype(F32) + first

    def grad(q):
        lrow = sublanes(rowl[pl.ds(q, 1), :])
        mine = sublanes(pid[q][0:1, :]) - place
        hit_sum = jnp.zeros((PAIRS, PAIRS), F32)
        dot_sum = jnp.zeros((PAIRS, PAIRS), F32)
        for r in range(NROW):
            at = slice(r * PAIRS, (r + 1) * PAIRS)
            s = scores[q, :, at]
            soft = 0.5 * (jnp.exp(s - lrow) + jnp.exp(s - coll[r : r + 1, :]))
            hit = (mine == float(r * PAIRS)).astype(F32)
            g = soft - hit
            hit_sum += s * hit
            dot_sum += s * g
            gb[pl.ds(pl.multiple_of(q * PAIRS, PAIRS), PAIRS), at] = g.astype(BF16)
        acc[0] += hit_sum
        acc[1] += dot_sum
        rows = gb[pl.ds(pl.multiple_of(q * PAIRS, PAIRS), PAIRS), :]
        pimg[q] = jnp.dot(rows, txt[...], preferred_element_type=F32).astype(BF16)

    def grad_line(start, length, where):
        @pl.loop(start, start + length)
        def _(i):
            grad(where(i))

    rg1n, rg2n, rf1n, rf2n = {}, {}, {}, {}
    slot = {2: 0, 1: 1, -1: 2, 0: 3}
    side = {1: 0, -1: 1}

    def scatter1(h):
        for j in STEPS:
            for d in DIRS:
                q = block(h, 2, j)
                rg1n[h, j, d] = net.send(
                    sub(pimg, q, h, d), rg1.at[h, slot[j], side[d]], gdev(h, d)
                )

    def scatter2(j):
        for h in (0, 1):
            for d in DIRS:
                q = block(h, d, j)
                got = rg1.at[h, slot[j], side[d]]
                net.recv(rg1n[h, j, d], got)
                part = sub(pimg, q, h, d)
                part[...] = (part[...].astype(F32) + got[...].astype(F32)).astype(BF16)
                rg2n[h, j, d] = net.send(
                    half(pimg, q, h), rg2.at[h, slot[j], side[d]], gdev(h, d)
                )

    def line_sum(h, j):
        for d in DIRS:
            net.recv(rg2n[h, j, d], rg2.at[h, slot[j], side[d]])
        total = half(pimg, block(h, 0, j), h)[...].astype(F32)
        for d in DIRS:
            total += rg2[h, slot[j], side[d]].astype(F32)
        return total

    grad_line(-1, 4, lambda i: rel(2, i))
    scatter1(0)
    grad_line(-1, 3, lambda i: rel(i, 2))
    scatter1(1)
    scatter2(2)
    grad_line(0, 4, lambda i: rel(2 * (i // 2) - 1, 2 * (i % 2) - 1))
    scatter2(1)
    scatter2(-1)
    grad_line(0, 2, lambda i: rel(2 * i - 1, 0))
    grad_line(0, 2, lambda i: rel(0, 2 * i - 1))
    scatter2(0)
    grad(rel(0, 0))

    mate_n, tx1n, tx2n = {}, {}, {}

    def text_product(dx):
        xx = (x + dx + 4) % 4
        at = pl.ds(pl.multiple_of(xx * 2 * PAIRS, 2 * PAIRS), 2 * PAIRS)
        prod = lax.dot_general(
            gb[:, at], img[...].reshape(NCOL * PAIRS, EMB), (((0,), (0,)), ((), ())),
            preferred_element_type=F32,
        )
        ptxt[at, :] = prod.astype(BF16)
        mate_n[dx] = net.send(ptxt.at[tblock(dx, 1 - c)], rc.at[xx], net.mate())

    def text_pair(dx):
        xx = (x + dx + 4) % 4
        net.recv(mate_n[dx], rc.at[xx])
        return ptxt[tblock(dx, c), :].astype(F32) + rc[xx].astype(F32)

    text_product(2)
    text_product(1)
    for h in (0, 1):
        rb[h, 0] = line_sum(h, 2).astype(BF16)
        for d in DIRS:
            at = pl.ds(0 if d == 1 else 32, 32)
            rf1n[h, d] = net.send(rb.at[h, 0, at], rf1.at[h, side[d]], fdev(h, d))
    ptxt[tblock(2, c), :] = text_pair(2).astype(BF16)
    for d in DIRS:
        tx1n[d] = net.send(ptxt.at[tsub(2, c, d)], rx1.at[side[d]], net.dev(dx=d))
    text_product(-1)
    for d in DIRS:
        ptxt[tblock(d, c), :] = text_pair(d).astype(BF16)
        net.recv(tx1n[d], rx1.at[side[d]])
        part = ptxt.at[tsub(d, c, d)]
        part[...] = (part[...].astype(F32) + rx1[side[d]].astype(F32)).astype(BF16)
        tx2n[d] = net.send(ptxt.at[tblock(d, c)], rx2.at[side[d]], net.dev(dx=d))
    text_product(0)
    for h in (0, 1):
        for d in DIRS:
            total = line_sum(h, d)
            net.recv(rf1n[h, d], rf1.at[h, side[d]])
            extra = rf1[h, side[d]].astype(F32)
            lo, hi = total[0:32], total[32:64]
            if d == 1:
                lo = lo + extra
            else:
                hi = hi + extra
            rb[h, 1 + side[d], 0:32] = lo.astype(BF16)
            rb[h, 1 + side[d], 32:64] = hi.astype(BF16)
            rf2n[h, d] = net.send(rb.at[h, 1 + side[d]], rf2.at[h, side[d]], fdev(h, d))

    total = text_pair(0)
    for d in DIRS:
        net.recv(tx2n[d], rx2.at[side[d]])
        total += rx2[side[d]].astype(F32)
    gtxt[...] = scale * total
    for h in (0, 1):
        total = line_sum(h, 0)
        for d in DIRS:
            net.recv(rf2n[h, d], rf2.at[h, side[d]])
            total += rf2[h, side[d]].astype(F32)
        gimg[pl.ds(64 * h, 64), :] = scale * total
    half_lse = (0.5 / NCOL) * jnp.sum(rowl[...].reshape(2, 8, PAIRS), axis=0) + (
        0.5 / NROW
    ) * coll[...]
    sums[0] = half_lse - jnp.sum(acc[0].reshape(16, 8, PAIRS), axis=0)
    sums[1] = jnp.sum(acc[1].reshape(16, 8, PAIRS), axis=0)
    net.finish()


def weight_kernel(
    pi, pt, dzi, dzt, tile, out, tot,
    ai, at, di, dt, w, r1, r2, q1, r3, q2, r4, s4, s2, send_sem, recv_sem,
):
    net = Net(send_sem, recv_sem)
    c = net.c
    place = (net.x, net.y, net.z)

    def dev(axis, d):
        return net.dev(**{("dx", "dy", "dz")[axis]: d})

    mine = pl.ds(pl.multiple_of(c * PAIRS, PAIRS), PAIRS)
    other = pl.ds(pl.multiple_of((1 - c) * PAIRS, PAIRS), PAIRS)
    keep = pl.ds(pl.multiple_of(c * HALF, 128), HALF)
    give = pl.ds(pl.multiple_of((1 - c) * HALF, 128), HALF)

    s4[0, net.x] = tile[...]
    net.barrier()
    pair = []
    for src, dst in ((dzi.at[:, give], di), (dzt.at[:, give], dt), (pi, ai), (pt, at)):
        pair.append((net.send(src, dst.at[mine], net.mate()), dst))
    tot_n = {}

    def tot_send(axis):
        own = s4.at[axis, place[axis]]
        for d in (1, 2, 3):
            tot_n[axis, d] = net.send(own, own, dev(axis, d))

    def tot_recv(axis):
        for d in (1, 2, 3):
            net.recv(tot_n[axis, d], s4.at[axis, (place[axis] - d + 4) % 4])
        return s4[axis, 0] + s4[axis, 1] + s4[axis, 2] + s4[axis, 3]

    tot_send(0)
    ai[mine, :] = pi[...]
    at[mine, :] = pt[...]
    di[mine, :] = dzi[:, keep]
    dt[mine, :] = dzt[:, keep]
    w[DI + DT :, :] = jnp.zeros((128, HALF), BF16)
    for number, dst in pair:
        net.recv(number, dst.at[other])

    def product(left, right, base, tiles):
        @pl.loop(0, tiles)
        def _(i):
            cols = pl.ds(pl.multiple_of(i * 128, 128), 128)
            rows = pl.ds(pl.multiple_of(base + i * 128, 128), 128)
            w[rows, :] = lax.dot_general(
                left[:, cols], right[...], (((0,), (0,)), ((), ())), preferred_element_type=F32
            ).astype(BF16)

    product(ai, di, 0, DI // 128)
    product(at, dt, DI, DT // 128)

    orders = ((0, 1, 2), (1, 2, 0), (2, 0, 1))
    side = {1: 0, -1: 1}

    def near(axis, d):
        return (place[axis] + d + 4) % 4

    def rows_at(k, a, b=None, e=None, size=256):
        start = 1024 * k + 256 * a
        if b is not None:
            start = start + 64 * b
        if e is not None:
            start = start + 16 * e
        return pl.ds(pl.multiple_of(start, 16), size)

    def part(k, d, s):
        return pl.ds(pl.multiple_of(1024 * k + 256 * near(orders[k][0], d) + 128 * s, 128), 128)

    n1, n2, n3, n4 = {}, {}, {}, {}
    for k in range(3):
        for d in DIRS:
            n1[k, d] = net.send(
                w.at[part(k, 2, side[d])], r1.at[k, side[d]], dev(orders[k][0], d)
            )
    for k in range(3):
        for d in DIRS:
            net.recv(n1[k, d], r1.at[k, side[d]])
            got = part(k, d, side[d])
            w[got, :] = (w[got, :].astype(F32) + r1[k, side[d]].astype(F32)).astype(BF16)
            n2[k, d] = net.send(
                w.at[rows_at(k, near(orders[k][0], d))], r2.at[k, side[d]], dev(orders[k][0], d)
            )
    s4[1, net.y] = tot_recv(0)
    tot_send(1)
    for k in range(3):
        a_ax, b_ax, c_ax = orders[k]
        total = w[rows_at(k, place[a_ax]), :].astype(F32)
        for d in DIRS:
            net.recv(n2[k, d], r2.at[k, side[d]])
            total += r2[k, side[d]].astype(F32)
        q1[k] = total.astype(BF16)
        for d in (2, 1, 3):
            to = pl.ds(pl.multiple_of(64 * near(b_ax, d), 64), 64)
            n3[k, d] = net.send(q1.at[k, to], r3.at[k, d - 1], dev(b_ax, d))
    s4[2, net.z] = tot_recv(1)
    tot_send(2)
    for k in range(3):
        a_ax, b_ax, c_ax = orders[k]
        total = q1[k, pl.ds(pl.multiple_of(64 * place[b_ax], 64), 64), :].astype(F32)
        for d in (1, 3, 2):
            net.recv(n3[k, d], r3.at[k, d - 1])
            total += r3[k, d - 1].astype(F32)
        q2[k] = total.astype(BF16)
        for d in (2, 1, 3):
            to = pl.ds(pl.multiple_of(16 * near(c_ax, d), 16), 16)
            n4[k, d] = net.send(q2.at[k, to], r4.at[k, d - 1], dev(c_ax, d))

    m1, m2, m3, m4, mate_n = {}, {}, {}, {}, {}
    outc = out.at[c]
    s2[c] = tot_recv(2)
    tot_mate = net.send(s2.at[c], s2.at[c], net.mate())
    for k in range(3):
        a_ax, b_ax, c_ax = orders[k]
        total = q2[k, pl.ds(pl.multiple_of(16 * place[c_ax], 16), 16), :].astype(F32)
        for d in (1, 3, 2):
            net.recv(n4[k, d], r4.at[k, d - 1])
            total += r4[k, d - 1].astype(F32)
        own = rows_at(k, place[a_ax], place[b_ax], place[c_ax], 16)
        out[c, own, :] = total.astype(BF16)
        for d in (2, 1, 3):
            m1[k, d] = net.send(outc.at[own], outc.at[own], dev(c_ax, d))
    for k in range(3):
        a_ax, b_ax, c_ax = orders[k]
        for d in (1, 3, 2):
            net.recv(m1[k, d], outc.at[rows_at(k, place[a_ax], place[b_ax], near(c_ax, -d), 16)])
        own = rows_at(k, place[a_ax], place[b_ax], None, 64)
        for d in (2, 1, 3):
            m2[k, d] = net.send(outc.at[own], outc.at[own], dev(b_ax, d))

    def to_mate(name, rows):
        mate_n[name] = (net.send(outc.at[rows], outc.at[rows], net.mate()), rows)

    for k in range(3):
        a_ax, b_ax, c_ax = orders[k]
        for d in (1, 3, 2):
            net.recv(m2[k, d], outc.at[rows_at(k, place[a_ax], near(b_ax, -d), None, 64)])
        own = rows_at(k, place[a_ax])
        for d in DIRS:
            m3[k, d] = net.send(outc.at[own], outc.at[own], dev(a_ax, d))
        to_mate((k, 0), own)
    for k in range(3):
        for d in DIRS:
            net.recv(m3[k, d], outc.at[rows_at(k, near(orders[k][0], -d))])
            rows = part(k, -d, side[d])
            m4[k, d] = net.send(outc.at[rows], outc.at[rows], dev(orders[k][0], d))
        for d in DIRS:
            to_mate((k, d), rows_at(k, near(orders[k][0], -d)))
    for k in range(3):
        for d in DIRS:
            rows = part(k, 2, side[d])
            net.recv(m4[k, d], outc.at[rows])
            to_mate((k, d, 2), rows)
    for number, rows in mate_n.values():
        net.recv(number, out.at[1 - c, rows])
    net.recv(tot_mate, s2.at[1 - c])
    tot[...] = s2[0] + s2[1]
    net.finish()


def vmem(shape, dtype):
    return pltpu.VMEM(shape, dtype)


def spec():
    return pl.BlockSpec(memory_space=pltpu.VMEM)


def call_main(scale, eimg, etxt, pair):
    cols = NROW * PAIRS
    return pl.pallas_call(
        main_kernel,
        name="scores_and_gradients",
        out_shape=(
            jax.ShapeDtypeStruct((PAIRS, EMB), F32),
            jax.ShapeDtypeStruct((PAIRS, EMB), F32),
            jax.ShapeDtypeStruct((2, 8, PAIRS), F32),
        ),
        in_specs=[pl.BlockSpec(memory_space=pltpu.SMEM), spec(), spec(), spec()],
        out_specs=(spec(), spec(), spec()),
        scratch_shapes=[
            vmem((NCOL, PAIRS, EMB), BF16),
            vmem((cols, EMB), BF16),
            vmem((NCOL, 8, PAIRS), F32),
            vmem((NCOL, PAIRS, cols), F32),
            vmem((NCOL * PAIRS, cols), BF16),
            vmem((NCOL, PAIRS, EMB), BF16),
            vmem((cols, EMB), BF16),
            vmem((2, 4, 2, 32, EMB), BF16),
            vmem((2, 4, 2, 64, EMB), BF16),
            vmem((2, 3, 64, EMB), BF16),
            vmem((2, 2, 32, EMB), BF16),
            vmem((2, 2, 64, EMB), BF16),
            vmem((4, PAIRS, EMB), BF16),
            vmem((2, 64, EMB), BF16),
            vmem((2, PAIRS, EMB), BF16),
            vmem((8, cols), F32),
            vmem((8, cols), F32),
            vmem((NCOL, PAIRS), F32),
            vmem((4, NCOL, PAIRS), F32),
            vmem((4, NCOL, PAIRS), F32),
            vmem((NROW, PAIRS), F32),
            vmem((4, NROW, PAIRS), F32),
            vmem((2, NROW, PAIRS), F32),
            vmem((2, PAIRS, PAIRS), F32),
            pltpu.SemaphoreType.DMA((128,)),
            pltpu.SemaphoreType.DMA((128,)),
        ],
        compiler_params=pltpu.CompilerParams(
            collective_id=0, has_side_effects=True, vmem_limit_bytes=56 * 1024 * 1024
        ),
        cost_estimate=pl.CostEstimate(
            flops=16 * 10**9, bytes_accessed=4 * 10**6, transcendentals=8 * 10**6
        ),
    )(scale, eimg, etxt, pair)


def call_weights(pi, pt, dzi, dzt, tile):
    rows = DI + DT + 128
    return pl.pallas_call(
        weight_kernel,
        name="weight_gradients",
        out_shape=(
            jax.ShapeDtypeStruct((2, rows, HALF), BF16),
            jax.ShapeDtypeStruct((8, 128), F32),
        ),
        in_specs=[spec()] * 5,
        out_specs=(spec(), spec()),
        scratch_shapes=[
            vmem((2 * PAIRS, DI), BF16),
            vmem((2 * PAIRS, DT), BF16),
            vmem((2 * PAIRS, HALF), BF16),
            vmem((2 * PAIRS, HALF), BF16),
            vmem((rows, HALF), BF16),
            vmem((3, 2, 128, HALF), BF16),
            vmem((3, 2, 256, HALF), BF16),
            vmem((3, 256, HALF), BF16),
            vmem((3, 3, 64, HALF), BF16),
            vmem((3, 64, HALF), BF16),
            vmem((3, 3, 16, HALF), BF16),
            vmem((3, 4, 8, 128), F32),
            vmem((2, 8, 128), F32),
            pltpu.SemaphoreType.DMA((128,)),
            pltpu.SemaphoreType.DMA((128,)),
        ],
        compiler_params=pltpu.CompilerParams(
            collective_id=1, has_side_effects=True, vmem_limit_bytes=56 * 1024 * 1024
        ),
        cost_estimate=pl.CostEstimate(
            flops=10**9, bytes_accessed=16 * 10**6, transcendentals=0
        ),
    )(pi, pt, dzi, dzt, tile)


def embed(pooled, proj):
    z = jnp.dot(pooled, proj, preferred_element_type=F32)
    norms = jnp.sqrt(jnp.sum(z * z, axis=1, keepdims=True) + EPS)
    unit = z / norms
    return (unit, norms, unit.astype(BF16))


def normal_grad(grads, unit, norms):
    inner = jnp.sum(unit * grads, axis=1, keepdims=True)
    return ((grads - unit * inner) / norms).astype(BF16)


def pooled_grad(dz, proj):
    return lax.dot_general(
        dz, proj, (((1,), (1,)), ((), ())), preferred_element_type=F32
    ).astype(BF16)


def local(image_pooled, text_pooled, image_proj, text_proj, log_scale, pair_index):
    unit_img, norm_img, emb_img = embed(image_pooled, image_proj)
    unit_txt, norm_txt, emb_txt = embed(text_pooled, text_proj)
    scale = jnp.exp(log_scale)
    img_grads, txt_grads, sums = call_main(
        scale, emb_img, emb_txt, pair_index.astype(F32).reshape(1, PAIRS)
    )
    dz_img = normal_grad(img_grads, unit_img, norm_img)
    dz_txt = normal_grad(txt_grads, unit_txt, norm_txt)
    both = jnp.sum(sums, axis=(1, 2))
    lane = lax.broadcasted_iota(jnp.int32, (8, 128), 1)
    tile = jnp.where(lane == 0, both[0], jnp.where(lane == 1, both[1], 0.0))
    weights, totals = call_weights(image_pooled, text_pooled, dz_img, dz_txt, tile)
    dpi = pooled_grad(dz_img, image_proj)
    dpt = pooled_grad(dz_txt, text_proj)
    wide = jnp.concatenate([weights[0], weights[1]], axis=1).astype(F32)
    loss = totals[0, 0:1] / (PAIRS * NROW * NCOL)
    return (loss, dpi, dpt, wide[:DI], wide[DI : DI + DT], totals[0, 1:2])


def solution(mesh):
    return jax.shard_map(
        local,
        mesh=mesh,
        in_specs=(
            P(("row", "col"), None),
            P(("col", "row"), None),
            P(),
            P(),
            P(),
            P(("row", "col")),
        ),
        out_specs=(P(), P(("row", "col"), None), P(("col", "row"), None), P(), P(), P()),
        check_vma=False,
    )
```

time: 561 us -> 213 us (0.38)
  waiting for transfers between devices: 254 us -> 0 us
  blocking collectives: 186 us -> 0 us
  Pallas kernels: 0 us -> 159 us
  matrix products: 51.5 us -> 9.31 us
  between operations: 18.3 us -> 3.24 us
  local copies, waits for them, and re-layouts: 24.2 us -> 18.4 us
    pallas_call x0 -> x2, Pallas kernels: none -> 159 us  [the longest x1 93.4 us: call_main(): pl.pallas_call(main_kernel, name='scores_and_gradients', out_shape=(jax.S...]
    psum x3 -> x0, blocking collectives: 108 us -> none  [the longest x1 66.4 us: local(): lax.psum((weight_term(image_pooled, dz_img), weight_term(text_pooled, dz_...]
    psum x1 -> x0, waiting for transfers between devices: 96.1 us -> none  [local(): lax.psum((weight_term(image_pooled, dz_img), weight_term(text_pooled, dz_...]
    reduce_scatter x2 -> x0, waiting for transfers between devices: 94.5 us -> none  [the longest x1 77.1 us: local(): lax.psum_scatter((scale * jnp.dot(piece, txt_block, preferred_element_typ...]
    all_gather x2 -> x0, waiting for transfers between devices: 63.8 us -> none  [the longest x1 59.4 us: local(): lax.all_gather(emb_img, 'col', axis=0, tiled=True)]
    pmax x2 -> x0, blocking collectives: 58.4 us -> none  [the longest x1 32 us: local(): row_peak = lax.pmax(row_peak, 'col')]
    dot_general x9 -> x4, matrix products: 51.5 us -> 9.31 us  [the longest x2 6.38 us: pooled_grad(): lax.dot_general(dz, proj, (((1,), (1,)), ((), ())), preferred_element_typ...]
    all_gather x1 -> x0, blocking collectives: 19.7 us -> none  [local(): lax.all_gather(pair_index, 'col', axis=0, tiled=True)]
  transfers between devices with their start and end apart: 5 -> 0, of which waited for: 5 -> 0; matrix products, arithmetic and copies ran while one was open for 5% -> 0% of each run, Pallas kernels for 0% -> 0%
where the time goes in v1:
time: 213 us; the launch traced here: 212 us
  Pallas kernels  159 us (75%)
  other arithmetic  22.5 us (11%)
  local copies, waits for them, and re-layouts  18.4 us (9%)
  matrix products  9.31 us (4%)
  between operations  3.24 us (2%)
    pallas_call x1, Pallas kernels, call_main(): pl.pallas_call(main_kernel, name='scores_and_gradients', out_shape=(jax.S...  93.4 us
    pallas_call x1, Pallas kernels, call_weights(): pl.pallas_call(weight_kernel, name='weight_gradients', out_shape=(jax.Sha...  65.3 us
    convert_element_type x1, other arithmetic, local(): wide = jnp.concatenate([weights[0], weights[1]], axis=1).astype(F32)  10 us
    slice x2, local copies, waits for them, and re-layouts, local(): return (loss, dpi, dpt, wide[:DI], wide[DI:DI + DT], totals[0, 1:2])  8.79 us
    dot_general x2, matrix products, pooled_grad(): lax.dot_general(dz, proj, (((1,), (1,)), ((), ())), preferred_element_typ...  6.38 us
    unnamed x18, local copies, waits for them, and re-layouts  5.13 us

profile of v1, /device:TPU:1, one launch (start us, length us, event | category | flops | bytes accessed | tf_op | source)
XLA Modules:
  0.0 212.2 jit_solution(3880542858394921478)
XLA Ops:
  0.6 0.0 copy-start
  0.6 0.0 copy-start.6
  0.7 0.0 copy-start.3
  0.7 1.9 copy-done
  2.6 2.1 multiply_reduce_fusion.2
  4.6 0.0 copy-start.8
  4.7 0.8 fusion.1.etxt
  5.5 0.0 copy-done.6
  5.5 0.0 copy-done.3
  5.5 0.9 multiply_reduce_fusion.3
  6.4 0.8 fusion.eimg
  7.9 0.0 copy-done.8
  7.9 0.5 convert_bitcast_fusion.pair
  8.4 93.4 %scores_and_gradients.1 = (f32[128,1280]{1,0:T(8,128)}, f32[128,1280]{1,0:T(8,128)}, f32[2,8,128]{2,1,0:T(8,128)}) custom-call(f32[1]{0:T(128)S(6)} %exp.3.scale_ref, bf16[128,1280]{1,0:T(8,128)(2,1)} %fusion.eimg, bf16[128,1280]{1,0:T(8,128)(2,1)} %fusion.1.etxt, f32[1,128]{1,0:T(1,128)} %convert_bitcast_fusion.pair), custom_call_target="tpu_custom_call" | custom-call | flops 16000000000 | bytes 4000000 | tf_op jit(solution)/shard_map/scores_and_gradients/pallas_call | solution.py:582
  101.9 0.0 copy-start.7
  101.9 1.3 multiply_reduce_fusion.1
  103.2 1.3 multiply_reduce_fusion
  104.5 2.4 %divide_convert_fusion = (bf16[128,1280]{1,0:T(8,128)(2,1)}, bf16[128,1280]{1,0:T(8,128)(2,1)}) fusion(f32[128,1280]{1,0:T(8,128)} %get-tuple-element.12, f32[128]{0:T(128)S(1)} %multiply_reduce_fusion, f32[128]{0:T(128)S(1)} %add_sqrt_fusion, f32[128,1280]{1,0:T(8,128)S(1)} %get-tuple-element.25, f32[128,1280]{1,0:T(8,128)} %get-tuple-element.11, ...), kind=kLoop, calls=%fused_computation.6 | loop fusion | flops 1638400 | bytes 3278848 | tf_op jit(solution)/shard_map/convert_element_type | solution.py:675
  106.9 0.0 copy-done.7
  106.9 0.1 reduce_sum.49
  107.0 0.6 fusion.3
  107.6 0.6 compare_select_fusion
  108.2 1.2 broadcast_select_fusion.tile
  109.5 65.3 %weight_gradients.1 = (bf16[2,3072,640]{2,1,0:T(8,128)(2,1)}, f32[8,128]{1,0:T(8,128)}) custom-call(bf16[128,1664]{1,0:T(8,128)(2,1)} %pi.1, bf16[128,1280]{1,0:T(8,128)(2,1)} %pt.1, bf16[128,1280]{1,0:T(8,128)(2,1)} %get-tuple-element.27.dzi, bf16[128,1280]{1,0:T(8,128)(2,1)} %get-tuple-element.26.dzt, f32[8,128]{1,0:T(8,128)} %broadcast_select_fusion.tile), custom_call_target="tpu_custom_call" | custom-call | flops 1000000000 | bytes 16000000 | tf_op jit(solution)/shard_map/weight_gradients/pallas_call | solution.py:631
  174.8 3.9 %slice_bitcast_fusion.1 = (bf16[3072,640]{1,0:T(8,128)(2,1)S(1)}, bf16[3072,640]{1,0:T(8,128)(2,1)S(1)}) fusion(bf16[2,3072,640]{2,1,0:T(8,128)(2,1)} %get-tuple-element.15), kind=kLoop, calls=%fused_computation.2 | loop fusion | bytes 15728640 | tf_op jit(solution)/shard_map/squeeze | solution.py:699
  178.7 0.0 copy-start.1
  178.7 0.0 copy-start.2
  178.8 1.9 copy-done.1
  180.6 1.3 copy-done.2
  181.9 3.2 %maximum_convert_fusion.1 = f32[1280,1280]{1,0:T(8,128)} fusion(bf16[3072,640]{1,0:T(8,128)(2,1)S(1)} %get-tuple-element.17, bf16[3072,640]{1,0:T(8,128)(2,1)S(1)} %get-tuple-element.16), kind=kLoop, calls=%fused_computation.3 | loop fusion | flops 6553600 | bytes 14417920 | tf_op jit(solution)/shard_map/slice | solution.py:701
  185.2 10.0 %maximum_convert_fusion = f32[3072,1280]{1,0:T(8,128)} fusion(bf16[3072,640]{1,0:T(8,128)(2,1)} %copy-done.2, bf16[3072,640]{1,0:T(8,128)(2,1)} %copy-done.1), kind=kLoop, calls=%fused_computation | loop fusion | flops 15728640 | bytes 23592960 | tf_op jit(solution)/shard_map/convert_element_type | solution.py:699
  195.2 0.0 copy-start.4
  195.2 7.5 %slice.32 = f32[1664,1280]{1,0:T(8,128)} slice(f32[3072,1280]{1,0:T(8,128)} %maximum_convert_fusion), slice={[0:1664], [0:1280]} | slice | bytes 17039360 | tf_op jit(solution)/shard_map/slice | solution.py:701
  202.7 0.0 copy-start.5
  202.7 1.3 fusion.2
  204.6 0.0 copy-done.4
  204.7 4.5 %convolution_convert_fusion = bf16[128,1664]{1,0:T(8,128)(2,1)} fusion(bf16[128,1280]{1,0:T(8,128)(2,1)S(1)} %copy-done.4, bf16[1664,1280]{1,0:T(8,128)(2,1)} %param.8), kind=kOutput, calls=%fused_computation.4 | convolution fusion | flops 545472512 | bytes 5013504 | tf_op jit(solution)/shard_map/dot_general | solution.py:679
  209.1 0.0 copy-done.5
  209.1 1.9 convolution_convert_fusion.1
  (3 shorter events, 0.0 us)
Async XLA Ops:
  0.6 1.9 copy-start
  0.6 4.9 %copy-start.6 = (bf16[128,1664]{1,0:T(8,128)(2,1)S(1)}, bf16[128,1664]{1,0:T(8,128)(2,1)}, u32[]{:S(2)}) copy-start(bf16[128,1664]{1,0:T(8,128)(2,1)} %pi.1) | copy-start | bytes 1277956
  0.7 4.8 %copy-start.3 = (bf16[1664,1280]{1,0:T(8,128)(2,1)S(1)}, bf16[1664,1280]{1,0:T(8,128)(2,1)}, u32[]{:S(2)}) copy-start(bf16[1664,1280]{1,0:T(8,128)(2,1)} %param.8) | copy-start | bytes 12779524
  4.6 3.3 %copy-start.8 = (s32[128]{0:T(128)S(1)}, s32[128]{0:T(128)}, u32[]{:S(2)}) copy-start(s32[128]{0:T(128)} %param.11) | copy-start | bytes 1540
  101.9 5.0 %copy-start.7 = (f32[2,8,128]{2,1,0:T(8,128)S(1)}, f32[2,8,128]{2,1,0:T(8,128)}, u32[]{:S(2)}) copy-start(f32[2,8,128]{2,1,0:T(8,128)} %get-tuple-element.13) | copy-start | bytes 24580
  178.7 1.9 copy-start.1
  178.7 3.2 %copy-start.2 = (bf16[3072,640]{1,0:T(8,128)(2,1)}, bf16[3072,640]{1,0:T(8,128)(2,1)S(1)}, u32[]{:S(2)}) copy-start(bf16[3072,640]{1,0:T(8,128)(2,1)S(1)} %get-tuple-element.17) | copy-start | bytes 11796484
  195.2 9.5 %copy-start.4 = (bf16[128,1280]{1,0:T(8,128)(2,1)S(1)}, bf16[128,1280]{1,0:T(8,128)(2,1)}, u32[]{:S(2)}) copy-start(bf16[128,1280]{1,0:T(8,128)(2,1)} %get-tuple-element.27.dzi) | copy-start | bytes 983044
  202.7 6.5 %copy-start.5 = (bf16[128,1280]{1,0:T(8,128)(2,1)S(1)}, bf16[128,1280]{1,0:T(8,128)(2,1)}, u32[]{:S(2)}) copy-start(bf16[128,1280]{1,0:T(8,128)(2,1)} %get-tuple-element.26.dzt) | copy-start | bytes 983044

commit v2 on v1

v2 whole, which is shorter than its diff:
```python
import functools

import jax
import jax.numpy as jnp
from jax import lax
from jax.experimental import pallas as pl
from jax.experimental.pallas import tpu as pltpu
from jax.sharding import PartitionSpec as P

EPS = 1e-06
MESH = pl.DeviceIdType.MESH
F32 = jnp.float32
BF16 = jnp.bfloat16
PAIRS = 128
NCOL = 16
NROW = 8
EMB = 1280
DI = 1664
DT = 1280
HALF = EMB // 2
DIRS = (1, -1)
STEPS = (2, 1, -1, 0)
WROWS = DI + DT + 128


class Net:
    def __init__(self, send_sem, recv_sem):
        self.send_sem, self.recv_sem = send_sem, recv_sem
        row, col = lax.axis_index("row"), lax.axis_index("col")
        self.x, self.c = row // 2, row % 2
        self.y, self.z = col // 4, col % 4
        self.count = 0
        self.started = []

    def dev(self, dx=0, dy=0, dz=0):
        return (
            2 * ((self.x + dx + 4) % 4) + self.c,
            4 * ((self.y + dy + 4) % 4) + (self.z + dz + 4) % 4,
        )

    def mate(self):
        return (2 * self.x + 1 - self.c, 4 * self.y + self.z)

    def greet(self):
        others = [self.mate()]
        for d in (1, 2, 3):
            others += [self.dev(dx=d), self.dev(dy=d), self.dev(dz=d)]
        self.others = len(others)
        for other in others:
            pl.semaphore_signal(
                pltpu.get_barrier_semaphore(), inc=1, device_id=other, device_id_type=MESH
            )

    def met(self):
        pl.semaphore_wait(pltpu.get_barrier_semaphore(), self.others)

    def copy(self, number, src, dst, device):
        return pltpu.make_async_remote_copy(
            src_ref=src,
            dst_ref=dst,
            send_sem=self.send_sem.at[number],
            recv_sem=self.recv_sem.at[number],
            device_id=device,
            device_id_type=MESH,
        )

    def send(self, src, dst, device):
        number = self.count
        self.count += 1
        copy = self.copy(number, src, dst, device)
        copy.start()
        self.started.append(copy)
        return number

    def recv(self, number, dst):
        self.copy(number, dst, dst, self.mate()).wait_recv()

    def finish(self):
        for copy in self.started:
            copy.wait_send()


def lanes(column):
    return jnp.transpose(jnp.broadcast_to(column, (PAIRS, PAIRS)))[0:1, :]


def sublanes(row):
    return jnp.transpose(jnp.broadcast_to(row, (PAIRS, PAIRS)))


def lse_over(parts):
    peak = functools.reduce(jnp.maximum, parts)
    return peak + jnp.log(sum(jnp.exp(p - peak) for p in parts))


def pick(i, options):
    value = options[0]
    for n in range(1, len(options)):
        value = jnp.where(i == n, options[n], value)
    return value


def kernel(
    scale_ref, pi, pt, wi_hbm, wt_hbm, pair, out, dpi, dpt, loss_ref, dscale_ref,
    img, txt, pid, scores, gb, pimg, ptxt,
    rg1, rg2, rb, rf1, rf2, rc, rx1, rx2,
    cmax, csum, rowl, rowz, rowy, coll, colx, colc, acc,
    wi, wt, unit_i, unit_t, norm_i, norm_t, turned, dz_i, dz_t, di, dt,
    w, r1, r2, q1, r3, q2, r4, fin, s4, s2,
    send_sem, recv_sem, local_sem,
):
    net = Net(send_sem, recv_sem)
    x, c, y, z = net.x, net.c, net.y, net.z
    me_col = 4 * y + z
    scale = scale_ref[0]
    load_i = pltpu.make_async_copy(wi_hbm, wi, local_sem.at[0])
    load_t = pltpu.make_async_copy(wt_hbm, wt, local_sem.at[1])
    load_i.start()
    load_t.start()
    net.greet()

    def axes(h):
        return ((y, z), (z, y))[h]

    def gdev(h, d):
        return net.dev(dy=d) if h == 0 else net.dev(dz=d)

    def fdev(h, d):
        return net.dev(dz=d) if h == 0 else net.dev(dy=d)

    def block(h, dg, df):
        g, f = axes(h)
        g, f = (g + dg + 4) % 4, (f + df + 4) % 4
        return 4 * g + f if h == 0 else 4 * f + g

    def half(ref, q, h):
        return ref.at[q, pl.ds(64 * h, 64)]

    def sub(ref, q, h, d):
        return ref.at[q, pl.ds(64 * h + (0 if d == 1 else 32), 32)]

    def rel(dy, dz):
        return 4 * ((y + dy + 4) % 4) + (z + dz + 4) % 4

    def tblock(dx, core):
        return pl.ds(pl.multiple_of((2 * ((x + dx + 4) % 4) + core) * PAIRS, PAIRS), PAIRS)

    def tsub(dx, core, d):
        start = (2 * ((x + dx + 4) % 4) + core) * PAIRS + (0 if d == 1 else 64)
        return pl.ds(pl.multiple_of(start, 64), 64)

    mine = pl.ds(pl.multiple_of(c * PAIRS, PAIRS), PAIRS)
    other = pl.ds(pl.multiple_of((1 - c) * PAIRS, PAIRS), PAIRS)
    keep = pl.ds(pl.multiple_of(c * HALF, 128), HALF)
    give = pl.ds(pl.multiple_of((1 - c) * HALF, 128), HALF)

    def embed(pooled, proj, unit, norm):
        value = jnp.dot(pooled[...], proj[...], preferred_element_type=F32)
        norms = jnp.sqrt(jnp.sum(value * value, axis=1, keepdims=True) + EPS)
        value = value / norms
        unit[...] = value
        norm[...] = jnp.broadcast_to(norms, norm.shape)
        return value.astype(BF16)

    pid[me_col] = jnp.broadcast_to(pair[...], (8, PAIRS))
    load_i.wait()
    img[me_col] = embed(pi, wi, unit_i, norm_i)
    net.met()

    f1, g1, f2, g3, g4 = {}, {}, {}, {}, {}
    x1, x2, cx = {}, {}, {}
    pz, py = {}, {}
    for h in (0, 1):
        for d in DIRS:
            part = half(img, me_col, h)
            f1[h, d] = net.send(part, part, fdev(h, d))
    for h in (0, 1):
        for d in DIRS:
            part = half(img, me_col, h)
            g1[h, d] = net.send(part, part, gdev(h, d))
    load_t.wait()
    txt[tblock(0, c), :] = embed(pt, wt, unit_t, norm_t)
    for d in DIRS:
        part = txt.at[tblock(0, c)]
        x1[d] = net.send(part, part, net.dev(dx=d))

    def to_mate(dx):
        part = txt.at[tblock(dx, c)]
        cx[dx] = net.send(part, part, net.mate())

    to_mate(0)
    for d in (1, 2, 3):
        pz[d] = net.send(pid.at[me_col], pid.at[me_col], net.dev(dz=d))
    turned[0:DT, mine] = jnp.transpose(pt[...])
    turned[DT:, mine] = jnp.transpose(pi[...])
    turn_n = net.send(turned.at[:, mine], turned.at[:, mine], net.mate())
    cmax[...] = jnp.full_like(cmax, -1e30)
    csum[...] = jnp.zeros_like(csum)
    acc[...] = jnp.zeros_like(acc)

    for h in (0, 1):
        for d in DIRS:
            q = block(h, 0, -d)
            net.recv(f1[h, d], half(img, q, h))
            f2[h, d] = net.send(sub(img, q, h, d), sub(img, q, h, d), fdev(h, d))
            for e in DIRS:
                g3[h, -d, e] = net.send(half(img, q, h), half(img, q, h), gdev(h, e))

    def pass_on(h, j, d):
        q = block(h, -d, j)
        net.recv(g1[h, d] if j == 0 else g3[h, j, d], half(img, q, h))
        g4[h, j, d] = net.send(sub(img, q, h, d), sub(img, q, h, d), gdev(h, d))

    for h in (0, 1):
        for d in DIRS:
            pass_on(h, 0, d)
    for d in DIRS:
        net.recv(x1[d], txt.at[tblock(-d, c)])
        part = txt.at[tsub(-d, c, d)]
        x2[d] = net.send(part, part, net.dev(dx=d))
        to_mate(-d)
    for h in (0, 1):
        q = block(h, 0, 2)
        for d in DIRS:
            net.recv(f2[h, d], sub(img, q, h, d))
        for d in DIRS:
            g3[h, 2, d] = net.send(half(img, q, h), half(img, q, h), gdev(h, d))
    for d in (1, 2, 3):
        net.recv(pz[d], pid.at[rel(0, -d)])
    for d in (1, 2, 3):
        line = pid.at[pl.ds(4 * y, 4)]
        py[d] = net.send(line, line, net.dev(dy=d))
    for d in DIRS:
        net.recv(x2[d], txt.at[tsub(2, c, d)])
    to_mate(2)
    for dx in (0, 1, -1, 2):
        net.recv(cx[dx], txt.at[tblock(dx, 1 - c)])

    def score(qa, qb):
        left = jnp.concatenate([img[qa], img[qb]], axis=0)
        s2q = scale * lax.dot_general(
            left, txt[...], (((1,), (1,)), ((), ())), preferred_element_type=F32
        )
        for q, s in ((qa, s2q[:PAIRS]), (qb, s2q[PAIRS:])):
            scores[q] = s
            peak = jnp.max(s, axis=1, keepdims=True)
            total = jnp.sum(jnp.exp(s - peak), axis=1, keepdims=True)
            rowl[pl.ds(q, 1), :] = lanes(peak + jnp.log(total))
        s3 = s2q.reshape(2 * PAIRS // 8, 8, s2q.shape[1])
        old = cmax[...]
        new = jnp.maximum(old, jnp.max(s3, axis=0))
        csum[...] = csum[...] * jnp.exp(old - new) + jnp.sum(jnp.exp(s3 - new[None]), axis=0)
        cmax[...] = new

    def in_pairs(work, *pairs):
        if len(pairs) == 1:
            (a, b), (e, f) = pairs[0]
            work(rel(a, b), rel(e, f))
            return

        @pl.loop(0, len(pairs))
        def _(i):
            a, b, e, f = (pick(i, [p[m][n] for p in pairs]) for m in (0, 1) for n in (0, 1))
            work(rel(a, b), rel(e, f))

    def last_hop(j):
        for h in (0, 1):
            for d in DIRS:
                net.recv(g4[h, j, d], sub(img, block(h, 2, j), h, d))

    in_pairs(score, ((0, 0), (0, 1)))
    for h in (0, 1):
        for j in (1, -1):
            for d in DIRS:
                pass_on(h, j, d)
    in_pairs(score, ((0, -1), (1, 0)), ((-1, 0), (1, 1)))
    for h in (0, 1):
        for d in DIRS:
            pass_on(h, 2, d)
    last_hop(0)
    in_pairs(score, ((1, -1), (-1, 1)), ((-1, -1), (2, 0)))
    last_hop(1)
    last_hop(-1)
    in_pairs(score, ((0, 2), (2, 1)), ((1, 2), (2, -1)))
    last_hop(2)
    in_pairs(score, ((-1, 2), (2, 2)))

    rz, ry, lx = {}, {}, {}
    rowz[z] = rowl[...]
    for d in (1, 2, 3):
        rz[d] = net.send(rowz.at[z], rowz.at[z], net.dev(dz=d))
    peak = jnp.max(cmax[...], axis=0, keepdims=True)
    lcol = peak + jnp.log(jnp.sum(csum[...] * jnp.exp(cmax[...] - peak), axis=0, keepdims=True))
    for r in range(NROW):
        coll[r : r + 1, :] = lcol[:, r * PAIRS : (r + 1) * PAIRS]
    colx[x] = coll[...]
    for d in (1, 2, 3):
        lx[d] = net.send(colx.at[x], colx.at[x], net.dev(dx=d))
    for d in (1, 2, 3):
        net.recv(rz[d], rowz.at[(z - d + 4) % 4])
    rowy[y] = lse_over([rowz[i] for i in range(4)])
    for d in (1, 2, 3):
        ry[d] = net.send(rowy.at[y], rowy.at[y], net.dev(dy=d))
    for d in (1, 2, 3):
        net.recv(lx[d], colx.at[(x - d + 4) % 4])
    colc[c] = lse_over([colx[i] for i in range(4)])
    lc = net.send(colc.at[c], colc.at[c], net.mate())
    for d in (1, 2, 3):
        line = pid.at[pl.ds(4 * ((y - d + 4) % 4), 4)]
        net.recv(py[d], line)
    for d in (1, 2, 3):
        net.recv(ry[d], rowy.at[(y - d + 4) % 4])
    rowl[...] = lse_over([rowy[i] for i in range(4)])
    net.recv(lc, colc.at[1 - c])
    coll[...] = lse_over([colc[i] for i in range(2)])

    first = (me_col * NROW * PAIRS).astype(F32)
    place = lax.broadcasted_iota(jnp.int32, (PAIRS, PAIRS), 1).astype(F32) + first

    def grad(qa, qb):
        rows = []
        for q in (qa, qb):
            lrow = sublanes(rowl[pl.ds(q, 1), :])
            target = sublanes(pid[q][0:1, :]) - place
            hit_sum = jnp.zeros((PAIRS, PAIRS), F32)
            dot_sum = jnp.zeros((PAIRS, PAIRS), F32)
            here = pl.ds(pl.multiple_of(q * PAIRS, PAIRS), PAIRS)
            for r in range(NROW):
                at = slice(r * PAIRS, (r + 1) * PAIRS)
                s = scores[q, :, at]
                soft = 0.5 * (jnp.exp(s - lrow) + jnp.exp(s - coll[r : r + 1, :]))
                hit = (target == float(r * PAIRS)).astype(F32)
                g = soft - hit
                hit_sum += s * hit
                dot_sum += s * g
                gb[here, at] = g.astype(BF16)
            acc[0] += hit_sum
            acc[1] += dot_sum
            rows.append(gb[here, :])
        prod = jnp.dot(jnp.concatenate(rows, axis=0), txt[...], preferred_element_type=F32)
        pimg[qa] = prod[:PAIRS].astype(BF16)
        pimg[qb] = prod[PAIRS:].astype(BF16)

    rg1n, rg2n, rf1n, rf2n = {}, {}, {}, {}
    slot = {2: 0, 1: 1, -1: 2, 0: 3}
    side = {1: 0, -1: 1}

    def scatter1(h, *js):
        for j in js:
            for d in DIRS:
                q = block(h, 2, j)
                rg1n[h, j, d] = net.send(
                    sub(pimg, q, h, d), rg1.at[h, slot[j], side[d]], gdev(h, d)
                )

    def scatter2(j):
        for h in (0, 1):
            for d in DIRS:
                q = block(h, d, j)
                got = rg1.at[h, slot[j], side[d]]
                net.recv(rg1n[h, j, d], got)
                part = sub(pimg, q, h, d)
                part[...] = (part[...].astype(F32) + got[...].astype(F32)).astype(BF16)
                rg2n[h, j, d] = net.send(
                    half(pimg, q, h), rg2.at[h, slot[j], side[d]], gdev(h, d)
                )

    def line_sum(h, j):
        for d in DIRS:
            net.recv(rg2n[h, j, d], rg2.at[h, slot[j], side[d]])
        total = half(pimg, block(h, 0, j), h)[...].astype(F32)
        for d in DIRS:
            total += rg2[h, slot[j], side[d]].astype(F32)
        return total

    in_pairs(grad, ((2, 2), (2, 1)))
    scatter1(0, 2, 1)
    in_pairs(grad, ((2, -1), (2, 0)), ((1, 2), (-1, 2)))
    scatter1(0, -1, 0)
    scatter1(1, 2, 1, -1)
    in_pairs(grad, ((0, 2), (1, 1)), ((1, -1), (-1, 1)))
    scatter1(1, 0)
    scatter2(2)
    in_pairs(grad, ((-1, -1), (1, 0)), ((0, 1), (-1, 0)))
    scatter2(1)
    scatter2(-1)
    in_pairs(grad, ((0, -1), (0, 0)))
    scatter2(0)

    mate_n, tx1n, tx2n = {}, {}, {}

    def text_product(dx):
        xx = (x + dx + 4) % 4
        at = pl.ds(pl.multiple_of(xx * 2 * PAIRS, 2 * PAIRS), 2 * PAIRS)
        prod = lax.dot_general(
            gb[:, at], img[...].reshape(NCOL * PAIRS, EMB), (((0,), (0,)), ((), ())),
            preferred_element_type=F32,
        )
        ptxt[at, :] = prod.astype(BF16)
        mate_n[dx] = net.send(ptxt.at[tblock(dx, 1 - c)], rc.at[xx], net.mate())

    def text_pair(dx):
        xx = (x + dx + 4) % 4
        net.recv(mate_n[dx], rc.at[xx])
        return ptxt[tblock(dx, c), :].astype(F32) + rc[xx].astype(F32)

    text_product(2)
    text_product(1)
    for h in (0, 1):
        rb[h, 0] = line_sum(h, 2).astype(BF16)
        for d in DIRS:
            at = pl.ds(0 if d == 1 else 32, 32)
            rf1n[h, d] = net.send(rb.at[h, 0, at], rf1.at[h, side[d]], fdev(h, d))
    ptxt[tblock(2, c), :] = text_pair(2).astype(BF16)
    for d in DIRS:
        tx1n[d] = net.send(ptxt.at[tsub(2, c, d)], rx1.at[side[d]], net.dev(dx=d))
    text_product(-1)
    for d in DIRS:
        ptxt[tblock(d, c), :] = text_pair(d).astype(BF16)
        net.recv(tx1n[d], rx1.at[side[d]])
        part = ptxt.at[tsub(d, c, d)]
        part[...] = (part[...].astype(F32) + rx1[side[d]].astype(F32)).astype(BF16)
        tx2n[d] = net.send(ptxt.at[tblock(d, c)], rx2.at[side[d]], net.dev(dx=d))
    text_product(0)
    for h in (0, 1):
        for d in DIRS:
            total = line_sum(h, d)
            net.recv(rf1n[h, d], rf1.at[h, side[d]])
            extra = rf1[h, side[d]].astype(F32)
            lo, hi = total[0:32], total[32:64]
            if d == 1:
                lo = lo + extra
            else:
                hi = hi + extra
            rb[h, 1 + side[d], 0:32] = lo.astype(BF16)
            rb[h, 1 + side[d], 32:64] = hi.astype(BF16)
            rf2n[h, d] = net.send(rb.at[h, 1 + side[d]], rf2.at[h, side[d]], fdev(h, d))

    where = (x, y, z)

    def dev(axis, d):
        return net.dev(**{("dx", "dy", "dz")[axis]: d})

    tot_n = {}

    def tot_send(axis):
        own = s4.at[axis, where[axis]]
        for d in (1, 2, 3):
            tot_n[axis, d] = net.send(own, own, dev(axis, d))

    def tot_recv(axis):
        for d in (1, 2, 3):
            net.recv(tot_n[axis, d], s4.at[axis, (where[axis] - d + 4) % 4])
        return s4[axis, 0] + s4[axis, 1] + s4[axis, 2] + s4[axis, 3]

    half_lse = (0.5 / NCOL) * jnp.sum(rowl[...].reshape(2, 8, PAIRS), axis=0) + (
        0.5 / NROW
    ) * coll[...]
    s4[0, x, 0:8] = half_lse - jnp.sum(acc[0].reshape(16, 8, PAIRS), axis=0)
    s4[0, x, 8:16] = jnp.sum(acc[1].reshape(16, 8, PAIRS), axis=0)
    tot_send(0)

    def normal_grad(grads, unit, norm, dz, halves):
        u = unit[...]
        inner = jnp.sum(u * grads, axis=1, keepdims=True)
        dz[...] = ((grads - u * inner) / norm[:, 0:1]).astype(BF16)
        number = net.send(dz.at[:, give], halves.at[mine], net.mate())
        halves[mine, :] = dz[:, keep]
        return number

    total = text_pair(0)
    for d in DIRS:
        net.recv(tx2n[d], rx2.at[side[d]])
        total += rx2[side[d]].astype(F32)
    dt_n = normal_grad(scale * total, unit_t, norm_t, dz_t, dt)
    w[DI + DT :, :] = jnp.zeros((WROWS - DI - DT, HALF), BF16)
    net.recv(turn_n, turned.at[:, other])

    orders = ((0, 1, 2), (1, 2, 0), (2, 0, 1))

    def near(axis, d):
        return (where[axis] + d + 4) % 4

    def rows_at(k, a, b=None, e=None, size=256):
        start = 1024 * k + 256 * a
        if b is not None:
            start = start + 64 * b
        if e is not None:
            start = start + 16 * e
        return pl.ds(pl.multiple_of(start, 16), size)

    def part_at(k, d, s):
        return pl.ds(pl.multiple_of(1024 * k + 256 * near(orders[k][0], d) + 128 * s, 128), 128)

    def weights(first_row, rows, right):
        @pl.loop(0, rows // 128)
        def _(i):
            at = pl.ds(pl.multiple_of(first_row + i * 128, 128), 128)
            w[at, :] = jnp.dot(turned[at, :], right[...], preferred_element_type=F32).astype(BF16)

    n1, n2, n3, n4 = {}, {}, {}, {}

    def reduce1(k):
        for d in DIRS:
            n1[k, d] = net.send(
                w.at[part_at(k, 2, side[d])], r1.at[k, side[d]], dev(orders[k][0], d)
            )

    net.recv(dt_n, dt.at[other])
    weights(0, DT, dt)
    reduce1(0)

    halves = []
    for h in (0, 1):
        total = line_sum(h, 0)
        for d in DIRS:
            net.recv(rf2n[h, d], rf2.at[h, side[d]])
            total += rf2[h, side[d]].astype(F32)
        halves.append(scale * total)
    di_n = normal_grad(jnp.concatenate(halves, axis=0), unit_i, norm_i, dz_i, di)
    net.recv(di_n, di.at[other])
    weights(DT, DI, di)
    reduce1(1)
    reduce1(2)

    def pooled_grad(dz, proj, result, rows):
        @pl.loop(0, rows // 128)
        def _(i):
            at = pl.ds(pl.multiple_of(i * 128, 128), 128)
            result[:, at] = lax.dot_general(
                dz[...], proj[at, :], (((1,), (1,)), ((), ())), preferred_element_type=F32
            ).astype(BF16)

    for k in range(3):
        for d in DIRS:
            net.recv(n1[k, d], r1.at[k, side[d]])
            got = part_at(k, d, side[d])
            w[got, :] = (w[got, :].astype(F32) + r1[k, side[d]].astype(F32)).astype(BF16)
            n2[k, d] = net.send(
                w.at[rows_at(k, near(orders[k][0], d))], r2.at[k, side[d]], dev(orders[k][0], d)
            )
    s4[1, y] = tot_recv(0)
    tot_send(1)
    pooled_grad(dz_i, wi, dpi, DI)
    pooled_grad(dz_t, wt, dpt, DT)
    for k in range(3):
        a_ax, b_ax, c_ax = orders[k]
        total = w[rows_at(k, where[a_ax]), :].astype(F32)
        for d in DIRS:
            net.recv(n2[k, d], r2.at[k, side[d]])
            total += r2[k, side[d]].astype(F32)
        q1[k] = total.astype(BF16)
        for d in (2, 1, 3):
            to = pl.ds(pl.multiple_of(64 * near(b_ax, d), 64), 64)
            n3[k, d] = net.send(q1.at[k, to], r3.at[k, d - 1], dev(b_ax, d))
    s4[2, z] = tot_recv(1)
    tot_send(2)
    for k in range(3):
        a_ax, b_ax, c_ax = orders[k]
        total = q1[k, pl.ds(pl.multiple_of(64 * where[b_ax], 64), 64), :].astype(F32)
        for d in (1, 3, 2):
            net.recv(n3[k, d], r3.at[k, d - 1])
            total += r3[k, d - 1].astype(F32)
        q2[k] = total.astype(BF16)
        for d in (2, 1, 3):
            to = pl.ds(pl.multiple_of(16 * near(c_ax, d), 16), 16)
            n4[k, d] = net.send(q2.at[k, to], r4.at[k, d - 1], dev(c_ax, d))
    s2[c] = tot_recv(2)
    tot_mate = net.send(s2.at[c], s2.at[c], net.mate())

    m1, m2, m3, m4, back = {}, {}, {}, {}, {}

    def cut(rows):
        return out.at[rows, keep]

    for k in range(3):
        a_ax, b_ax, c_ax = orders[k]
        total = q2[k, pl.ds(pl.multiple_of(16 * where[c_ax], 16), 16), :].astype(F32)
        for d in (1, 3, 2):
            net.recv(n4[k, d], r4.at[k, d - 1])
            total += r4[k, d - 1].astype(F32)
        fin[k] = total.astype(BF16)
        own = cut(rows_at(k, where[a_ax], where[b_ax], where[c_ax], 16))
        for d in (2, 1, 3):
            m1[k, d] = net.send(fin.at[k], own, dev(c_ax, d))
        back[k] = pltpu.make_async_copy(fin.at[k], own, local_sem.at[2 + k])
        back[k].start()
    for k in range(3):
        a_ax, b_ax, c_ax = orders[k]
        back[k].wait()
        for d in (1, 3, 2):
            net.recv(m1[k, d], cut(rows_at(k, where[a_ax], where[b_ax], near(c_ax, -d), 16)))
        own = cut(rows_at(k, where[a_ax], where[b_ax], None, 64))
        for d in (2, 1, 3):
            m2[k, d] = net.send(own, own, dev(b_ax, d))

    over = []

    def to_mate(rows):
        over.append((net.send(cut(rows), cut(rows), net.mate()), rows))

    for k in range(3):
        a_ax, b_ax, c_ax = orders[k]
        for d in (1, 3, 2):
            net.recv(m2[k, d], cut(rows_at(k, where[a_ax], near(b_ax, -d), None, 64)))
        rows = rows_at(k, where[a_ax])
        for d in DIRS:
            m3[k, d] = net.send(cut(rows), cut(rows), dev(a_ax, d))
        to_mate(rows)
    for k in range(3):
        for d in DIRS:
            net.recv(m3[k, d], cut(rows_at(k, near(orders[k][0], -d))))
            rows = part_at(k, -d, side[d])
            m4[k, d] = net.send(cut(rows), cut(rows), dev(orders[k][0], d))
        for d in DIRS:
            to_mate(rows_at(k, near(orders[k][0], -d)))
    for k in range(3):
        for d in DIRS:
            rows = part_at(k, 2, side[d])
            net.recv(m4[k, d], cut(rows))
            to_mate(rows)
    net.recv(tot_mate, s2.at[1 - c])
    totals = s2[0] + s2[1]
    loss_ref[0] = jnp.sum(totals[0:8]) * (1.0 / (PAIRS * NROW * NCOL))
    dscale_ref[0] = jnp.sum(totals[8:16])
    for number, rows in over:
        net.recv(number, out.at[rows, give])
    net.finish()


def local(image_pooled, text_pooled, image_proj, text_proj, log_scale, pair_index):
    cols = NROW * PAIRS
    vmem = pltpu.VMEM
    held = pl.BlockSpec(memory_space=pltpu.VMEM)
    scalar = pl.BlockSpec(memory_space=pltpu.SMEM)
    far = pl.BlockSpec(memory_space=pl.ANY)
    weights, dpi, dpt, loss, dscale = pl.pallas_call(
        kernel,
        name="contrastive_loss",
        out_shape=(
            jax.ShapeDtypeStruct((WROWS, EMB), BF16),
            jax.ShapeDtypeStruct((PAIRS, DI), BF16),
            jax.ShapeDtypeStruct((PAIRS, DT), BF16),
            jax.ShapeDtypeStruct((1,), F32),
            jax.ShapeDtypeStruct((1,), F32),
        ),
        in_specs=[scalar, held, held, far, far, held],
        out_specs=(far, held, held, scalar, scalar),
        scratch_shapes=[
            vmem((NCOL, PAIRS, EMB), BF16),
            vmem((cols, EMB), BF16),
            vmem((NCOL, 8, PAIRS), F32),
            vmem((NCOL, PAIRS, cols), F32),
            vmem((NCOL * PAIRS, cols), BF16),
            vmem((NCOL, PAIRS, EMB), BF16),
            vmem((cols, EMB), BF16),
            vmem((2, 4, 2, 32, EMB), BF16),
            vmem((2, 4, 2, 64, EMB), BF16),
            vmem((2, 3, 64, EMB), BF16),
            vmem((2, 2, 32, EMB), BF16),
            vmem((2, 2, 64, EMB), BF16),
            vmem((4, PAIRS, EMB), BF16),
            vmem((2, 64, EMB), BF16),
            vmem((2, PAIRS, EMB), BF16),
            vmem((8, cols), F32),
            vmem((8, cols), F32),
            vmem((NCOL, PAIRS), F32),
            vmem((4, NCOL, PAIRS), F32),
            vmem((4, NCOL, PAIRS), F32),
            vmem((NROW, PAIRS), F32),
            vmem((4, NROW, PAIRS), F32),
            vmem((2, NROW, PAIRS), F32),
            vmem((2, PAIRS, PAIRS), F32),
            vmem((DI, EMB), BF16),
            vmem((DT, EMB), BF16),
            vmem((PAIRS, EMB), F32),
            vmem((PAIRS, EMB), F32),
            vmem((PAIRS, 128), F32),
            vmem((PAIRS, 128), F32),
            vmem((DI + DT, 2 * PAIRS), BF16),
            vmem((PAIRS, EMB), BF16),
            vmem((PAIRS, EMB), BF16),
            vmem((2 * PAIRS, HALF), BF16),
            vmem((2 * PAIRS, HALF), BF16),
            vmem((WROWS, HALF), BF16),
            vmem((3, 2, 128, HALF), BF16),
            vmem((3, 2, 256, HALF), BF16),
            vmem((3, 256, HALF), BF16),
            vmem((3, 3, 64, HALF), BF16),
            vmem((3, 64, HALF), BF16),
            vmem((3, 3, 16, HALF), BF16),
            vmem((3, 16, HALF), BF16),
            vmem((3, 4, 16, 128), F32),
            vmem((2, 16, 128), F32),
            pltpu.SemaphoreType.DMA((256,)),
            pltpu.SemaphoreType.DMA((256,)),
            pltpu.SemaphoreType.DMA((8,)),
        ],
        compiler_params=pltpu.CompilerParams(
            collective_id=0, has_side_effects=True, vmem_limit_bytes=60 * 1024 * 1024
        ),
        cost_estimate=pl.CostEstimate(
            flops=19 * 10**9, bytes_accessed=24 * 10**6, transcendentals=8 * 10**6
        ),
    )(
        jnp.exp(log_scale), image_pooled, text_pooled, image_proj, text_proj,
        pair_index.astype(F32).reshape(1, PAIRS),
    )
    dwt = weights[:DT].astype(F32)
    dwi = weights[DT : DT + DI].astype(F32)
    return (loss, dpi, dpt, dwi, dwt, dscale)


def solution(mesh):
    return jax.shard_map(
        local,
        mesh=mesh,
        in_specs=(
            P(("row", "col"), None),
            P(("col", "row"), None),
            P(),
            P(),
            P(),
            P(("row", "col")),
        ),
        out_specs=(P(), P(("row", "col"), None), P(("col", "row"), None), P(), P(), P()),
        check_vma=False,
    )
```

time: 213 us -> 162 us (0.76)
  local copies, waits for them, and re-layouts: 18.4 us -> 1.75 us
  Pallas kernels: 159 us -> 145 us
  other arithmetic: 22.5 us -> 10.8 us
  matrix products: 9.31 us -> 0 us
    pallas_call x2 -> x1, Pallas kernels: 159 us -> 145 us  [local(): pl.pallas_call(kernel, name='contrastive_loss', out_shape=(jax.ShapeDtype...]
    slice x3 -> x0, local copies, waits for them, and re-layouts: 9.38 us -> none  [the longest x2 8.79 us: local(): return (loss, dpi, dpt, wide[:DI], wide[DI:DI + DT], totals[0, 1:2])]
    dot_general x4 -> x0, matrix products: 9.31 us -> none  [the longest x2 6.38 us: pooled_grad(): lax.dot_general(dz, proj, (((1,), (1,)), ((), ())), preferred_element_typ...]
    convert_element_type x4 -> x2, other arithmetic: 14.1 us -> 9.6 us  [the longest x1 5.51 us: local(): dwt = weights[:DT].astype(F32)]
    squeeze x1 -> x0, local copies, waits for them, and re-layouts: 3.9 us -> none  [local(): wide = jnp.concatenate([weights[0], weights[1]], axis=1).astype(F32)]
    unnamed x18 -> x8, local copies, waits for them, and re-layouts: 5.13 us -> 1.75 us
    slice x1 -> x0, other arithmetic: 3.25 us -> none  [local(): return (loss, dpi, dpt, wide[:DI], wide[DI:DI + DT], totals[0, 1:2])]
    reduce_sum x3 -> x0, other arithmetic: 2.72 us -> none  [the longest x2 2.62 us: normal_grad(): inner = jnp.sum(unit * grads, axis=1, keepdims=True)]
where the time goes in v2:
time: 162 us
  Pallas kernels  145 us (90%)
  other arithmetic  10.8 us (7%)
  between operations  4.78 us (3%)
  local copies, waits for them, and re-layouts  1.75 us (1%)
    pallas_call x1, Pallas kernels, local(): pl.pallas_call(kernel, name='contrastive_loss', out_shape=(jax.ShapeDtype...  145 us
    convert_element_type x1, other arithmetic, local(): dwt = weights[:DT].astype(F32)  5.51 us
    convert_element_type x1, other arithmetic, local(): dwi = weights[DT:DT + DI].astype(F32)  4.09 us

profile of v2, /device:TPU:1, one launch (start us, length us, event | category | flops | bytes accessed | tf_op | source)
XLA Modules:
  0.0 162.0 jit_solution(12308213779903537924)
XLA Ops:
  1.3 1.2 convert_bitcast_fusion.pair
  2.5 144.7 %contrastive_loss.1 = (bf16[3072,1280]{1,0:T(8,128)(2,1)}, bf16[128,1664]{1,0:T(8,128)(2,1)}, bf16[128,1280]{1,0:T(8,128)(2,1)}, f32[1]{0:T(128)}, f32[1]{0:T(128)}) custom-call(f32[1]{0:T(128)S(6)} %exp.3.scale_ref, bf16[128,1664]{1,0:T(8,128)(2,1)} %pi.1, bf16[128,1280]{1,0:T(8,128)(2,1)} %pt.1, bf16[1664,1280]{1,0:T(8,128)(2,1)} %wi_hbm.1, ...), custom_call_target="tpu_custom_call" | custom-call | flops 19000000512 | bytes 24000000 | tf_op jit(solution)/shard_map/contrastive_loss/pallas_call | solution.py:637
  147.2 0.0 copy-start
  147.2 5.5 %slice_convert_fusion.1 = f32[1280,1280]{1,0:T(8,128)} fusion(bf16[3072,1280]{1,0:T(8,128)(2,1)} %get-tuple-element.14), kind=kLoop, calls=%fused_computation.1 | loop fusion | flops 1638400 | bytes 9830400 | tf_op jit(solution)/shard_map/convert_element_type | solution.py:709
  152.7 0.3 copy-done
  152.9 0.0 copy-start.1
  152.9 0.0 copy-start.2
  152.9 4.1 %slice_convert_fusion = f32[1664,1280]{1,0:T(8,128)} fusion(bf16[3072,1280]{1,0:T(8,128)(2,1)S(1)} %copy-done), kind=kLoop, calls=%fused_computation | loop fusion | flops 2129920 | bytes 12779520 | tf_op jit(solution)/shard_map/convert_element_type | solution.py:710
  157.7 0.0 copy-done.1
  157.7 0.8 copy.18
  158.4 0.0 copy-done.2
  158.4 0.7 copy.19
Async XLA Ops:
  147.2 5.8 %copy-start = (bf16[3072,1280]{1,0:T(8,128)(2,1)S(1)}, bf16[3072,1280]{1,0:T(8,128)(2,1)}, u32[]{:S(2)}) copy-start(bf16[3072,1280]{1,0:T(8,128)(2,1)} %get-tuple-element.14) | copy-start | bytes 23592964
  152.9 4.7 %copy-start.1 = (bf16[128,1664]{1,0:T(8,128)(2,1)S(1)}, bf16[128,1664]{1,0:T(8,128)(2,1)}, u32[]{:S(2)}) copy-start(bf16[128,1664]{1,0:T(8,128)(2,1)} %get-tuple-element.23) | copy-start | bytes 1277956
  152.9 5.5 %copy-start.2 = (bf16[128,1280]{1,0:T(8,128)(2,1)S(1)}, bf16[128,1280]{1,0:T(8,128)(2,1)}, u32[]{:S(2)}) copy-start(bf16[128,1280]{1,0:T(8,128)(2,1)} %get-tuple-element.24) | copy-start | bytes 983044

commit v3 on v2

--- a/solution.py
+++ b/solution.py
@@ -112,7 +112,7 @@
     net = Net(send_sem, recv_sem)
     x, c, y, z = net.x, net.c, net.y, net.z
     me_col = 4 * y + z
-    scale = scale_ref[0]
+    scale = jnp.exp(jnp.full((8, 128), scale_ref[0], F32))[0:1, 0:1]
     load_i = pltpu.make_async_copy(wi_hbm, wi, local_sem.at[0])
     load_t = pltpu.make_async_copy(wt_hbm, wt, local_sem.at[1])
     load_i.start()
@@ -162,7 +162,7 @@
         norm[...] = jnp.broadcast_to(norms, norm.shape)
         return value.astype(BF16)
 
-    pid[me_col] = jnp.broadcast_to(pair[...], (8, PAIRS))
+    pid[me_col] = jnp.broadcast_to(pair[...].astype(F32), (8, PAIRS))
     load_i.wait()
     img[me_col] = embed(pi, wi, unit_i, norm_i)
     net.met()
@@ -375,16 +375,20 @@
 
     in_pairs(grad, ((2, 2), (2, 1)))
     scatter1(0, 2, 1)
-    in_pairs(grad, ((2, -1), (2, 0)), ((1, 2), (-1, 2)))
-    scatter1(0, -1, 0)
-    scatter1(1, 2, 1, -1)
-    in_pairs(grad, ((0, 2), (1, 1)), ((1, -1), (-1, 1)))
+    scatter1(1, 2)
+    in_pairs(grad, ((1, 2), (2, -1)))
+    scatter1(1, 1)
+    scatter1(0, -1)
+    in_pairs(grad, ((-1, 2), (2, 0)))
+    scatter1(1, -1)
+    scatter1(0, 0)
+    in_pairs(grad, ((0, 2), (1, 1)))
     scatter1(1, 0)
     scatter2(2)
-    in_pairs(grad, ((-1, -1), (1, 0)), ((0, 1), (-1, 0)))
+    in_pairs(grad, ((1, -1), (-1, 1)), ((-1, -1), (1, 0)))
     scatter2(1)
     scatter2(-1)
-    in_pairs(grad, ((0, -1), (0, 0)))
+    in_pairs(grad, ((0, 1), (-1, 0)), ((0, -1), (0, 0)))
     scatter2(0)
 
     mate_n, tx1n, tx2n = {}, {}, {}
@@ -498,17 +502,131 @@
             at = pl.ds(pl.multiple_of(first_row + i * 128, 128), 128)
             w[at, :] = jnp.dot(turned[at, :], right[...], preferred_element_type=F32).astype(BF16)
 
+    wide = [(k, 0, 384) for k in range(3)]
+    slim = [(k, 384, 256) for k in range(3)]
     n1, n2, n3, n4 = {}, {}, {}, {}
-
-    def reduce1(k):
-        for d in DIRS:
-            n1[k, d] = net.send(
-                w.at[part_at(k, 2, side[d])], r1.at[k, side[d]], dev(orders[k][0], d)
+    m1, m2, m3, m4, back = {}, {}, {}, {}, {}
+    over = []
+
+    def step(k, d):
+        return dev(orders[k][0], d)
+
+    def cut(ch, rows):
+        start = pl.multiple_of(c * HALF + ch[1], 128)
+        return out.at[rows, pl.ds(start, ch[2])]
+
+    def at_mate(ch, rows):
+        start = pl.multiple_of((1 - c) * HALF + ch[1], 128)
+        return out.at[rows, pl.ds(start, ch[2])]
+
+    def to_mate_w(ch, rows):
+        over.append((net.send(cut(ch, rows), cut(ch, rows), net.mate()), ch, rows))
+
+    def reduce1(ch):
+        k, lane = ch[0], pl.ds(ch[1], ch[2])
+        for d in DIRS:
+            n1[ch, d] = net.send(
+                w.at[part_at(k, 2, side[d]), lane], r1.at[k, side[d], :, lane], step(k, d)
             )
+
+    def reduce2(ch):
+        k, lane = ch[0], pl.ds(ch[1], ch[2])
+        for d in DIRS:
+            net.recv(n1[ch, d], r1.at[k, side[d], :, lane])
+            got = part_at(k, d, side[d])
+            w[got, lane] = (w[got, lane].astype(F32) + r1[k, side[d], :, lane].astype(F32)).astype(
+                BF16
+            )
+            n2[ch, d] = net.send(
+                w.at[rows_at(k, near(orders[k][0], d)), lane], r2.at[k, side[d], :, lane],
+                step(k, d),
+            )
+
+    def reduce3(ch):
+        k, lane = ch[0], pl.ds(ch[1], ch[2])
+        a_ax, b_ax, _ = orders[k]
+        total = w[rows_at(k, where[a_ax]), lane].astype(F32)
+        for d in DIRS:
+            net.recv(n2[ch, d], r2.at[k, side[d], :, lane])
+            total += r2[k, side[d], :, lane].astype(F32)
+        q1[k, :, lane] = total.astype(BF16)
+        for d in (2, 1, 3):
+            to = pl.ds(pl.multiple_of(64 * near(b_ax, d), 64), 64)
+            n3[ch, d] = net.send(q1.at[k, to, lane], r3.at[k, d - 1, :, lane], dev(b_ax, d))
+
+    def reduce4(ch):
+        k, lane = ch[0], pl.ds(ch[1], ch[2])
+        _, b_ax, c_ax = orders[k]
+        total = q1[k, pl.ds(pl.multiple_of(64 * where[b_ax], 64), 64), lane].astype(F32)
+        for d in (1, 3, 2):
+            net.recv(n3[ch, d], r3.at[k, d - 1, :, lane])
+            total += r3[k, d - 1, :, lane].astype(F32)
+        q2[k, :, lane] = total.astype(BF16)
+        for d in (2, 1, 3):
+            to = pl.ds(pl.multiple_of(16 * near(c_ax, d), 16), 16)
+            n4[ch, d] = net.send(q2.at[k, to, lane], r4.at[k, d - 1, :, lane], dev(c_ax, d))
+
+    def gather1(ch):
+        k, lane = ch[0], pl.ds(ch[1], ch[2])
+        a_ax, b_ax, c_ax = orders[k]
+        total = q2[k, pl.ds(pl.multiple_of(16 * where[c_ax], 16), 16), lane].astype(F32)
+        for d in (1, 3, 2):
+            net.recv(n4[ch, d], r4.at[k, d - 1, :, lane])
+            total += r4[k, d - 1, :, lane].astype(F32)
+        fin[k, :, lane] = total.astype(BF16)
+        own = cut(ch, rows_at(k, where[a_ax], where[b_ax], where[c_ax], 16))
+        for d in (2, 1, 3):
+            m1[ch, d] = net.send(fin.at[k, :, lane], own, dev(c_ax, d))
+        back[ch] = pltpu.make_async_copy(fin.at[k, :, lane], own, local_sem.at[2 + len(back)])
+        back[ch].start()
+
+    def gather2(ch):
+        k = ch[0]
+        a_ax, b_ax, c_ax = orders[k]
+        back[ch].wait()
+        for d in (1, 3, 2):
+            rows = rows_at(k, where[a_ax], where[b_ax], near(c_ax, -d), 16)
+            net.recv(m1[ch, d], cut(ch, rows))
+        own = cut(ch, rows_at(k, where[a_ax], where[b_ax], None, 64))
+        for d in (2, 1, 3):
+            m2[ch, d] = net.send(own, own, dev(b_ax, d))
+
+    def gather3(ch):
+        k = ch[0]
+        a_ax, b_ax, _ = orders[k]
+        for d in (1, 3, 2):
+            net.recv(m2[ch, d], cut(ch, rows_at(k, where[a_ax], near(b_ax, -d), None, 64)))
+        rows = rows_at(k, where[a_ax])
+        for d in DIRS:
+            m3[ch, d] = net.send(cut(ch, rows), cut(ch, rows), step(k, d))
+        to_mate_w(ch, rows)
+
+    def gather4(ch):
+        k = ch[0]
+        for d in DIRS:
+            net.recv(m3[ch, d], cut(ch, rows_at(k, near(orders[k][0], -d))))
+            rows = cut(ch, part_at(k, -d, side[d]))
+            m4[ch, d] = net.send(rows, rows, step(k, d))
+        for d in DIRS:
+            to_mate_w(ch, rows_at(k, near(orders[k][0], -d)))
+
+    def gather5(ch):
+        for d in DIRS:
+            rows = part_at(ch[0], 2, side[d])
+            net.recv(m4[ch, d], cut(ch, rows))
+            to_mate_w(ch, rows)
+
+    def each(work, *chunks):
+        for ch in chunks:
+            work(ch)
+
+    early = (wide[0], slim[0])
+    lead = (wide[1], wide[2])
+    tail = (slim[1], slim[2])
 
     net.recv(dt_n, dt.at[other])
     weights(0, DT, dt)
-    reduce1(0)
+    each(reduce1, *early)
 
     halves = []
     for h in (0, 1):
@@ -518,10 +636,11 @@
             total += rf2[h, side[d]].astype(F32)
         halves.append(scale * total)
     di_n = normal_grad(jnp.concatenate(halves, axis=0), unit_i, norm_i, dz_i, di)
+    each(reduce2, *early)
     net.recv(di_n, di.at[other])
     weights(DT, DI, di)
-    reduce1(1)
-    reduce1(2)
+    each(reduce1, *lead)
+    each(reduce1, *tail)
 
     def pooled_grad(dz, proj, result, rows):
         @pl.loop(0, rows // 128)
@@ -531,100 +650,43 @@
                 dz[...], proj[at, :], (((1,), (1,)), ((), ())), preferred_element_type=F32
             ).astype(BF16)
 
-    for k in range(3):
-        for d in DIRS:
-            net.recv(n1[k, d], r1.at[k, side[d]])
-            got = part_at(k, d, side[d])
-            w[got, :] = (w[got, :].astype(F32) + r1[k, side[d]].astype(F32)).astype(BF16)
-            n2[k, d] = net.send(
-                w.at[rows_at(k, near(orders[k][0], d))], r2.at[k, side[d]], dev(orders[k][0], d)
-            )
+    pooled_grad(dz_i, wi, dpi, DI)
+    each(reduce2, *lead)
+    each(reduce3, *early)
+    each(reduce2, *tail)
     s4[1, y] = tot_recv(0)
     tot_send(1)
-    pooled_grad(dz_i, wi, dpi, DI)
     pooled_grad(dz_t, wt, dpt, DT)
-    for k in range(3):
-        a_ax, b_ax, c_ax = orders[k]
-        total = w[rows_at(k, where[a_ax]), :].astype(F32)
-        for d in DIRS:
-            net.recv(n2[k, d], r2.at[k, side[d]])
-            total += r2[k, side[d]].astype(F32)
-        q1[k] = total.astype(BF16)
-        for d in (2, 1, 3):
-            to = pl.ds(pl.multiple_of(64 * near(b_ax, d), 64), 64)
-            n3[k, d] = net.send(q1.at[k, to], r3.at[k, d - 1], dev(b_ax, d))
+    each(reduce3, *lead)
+    each(reduce4, *early)
+    each(reduce3, *tail)
     s4[2, z] = tot_recv(1)
     tot_send(2)
-    for k in range(3):
-        a_ax, b_ax, c_ax = orders[k]
-        total = q1[k, pl.ds(pl.multiple_of(64 * where[b_ax], 64), 64), :].astype(F32)
-        for d in (1, 3, 2):
-            net.recv(n3[k, d], r3.at[k, d - 1])
-            total += r3[k, d - 1].astype(F32)
-        q2[k] = total.astype(BF16)
-        for d in (2, 1, 3):
-            to = pl.ds(pl.multiple_of(16 * near(c_ax, d), 16), 16)
-            n4[k, d] = net.send(q2.at[k, to], r4.at[k, d - 1], dev(c_ax, d))
+    each(reduce4, *lead)
+    each(gather1, *early)
+    each(reduce4, *tail)
     s2[c] = tot_recv(2)
     tot_mate = net.send(s2.at[c], s2.at[c], net.mate())
-
-    m1, m2, m3, m4, back = {}, {}, {}, {}, {}
-
-    def cut(rows):
-        return out.at[rows, keep]
-
-    for k in range(3):
-        a_ax, b_ax, c_ax = orders[k]
-        total = q2[k, pl.ds(pl.multiple_of(16 * where[c_ax], 16), 16), :].astype(F32)
-        for d in (1, 3, 2):
-            net.recv(n4[k, d], r4.at[k, d - 1])
-            total += r4[k, d - 1].astype(F32)
-        fin[k] = total.astype(BF16)
-        own = cut(rows_at(k, where[a_ax], where[b_ax], where[c_ax], 16))
-        for d in (2, 1, 3):
-            m1[k, d] = net.send(fin.at[k], own, dev(c_ax, d))
-        back[k] = pltpu.make_async_copy(fin.at[k], own, local_sem.at[2 + k])
-        back[k].start()
-    for k in range(3):
-        a_ax, b_ax, c_ax = orders[k]
-        back[k].wait()
-        for d in (1, 3, 2):
-            net.recv(m1[k, d], cut(rows_at(k, where[a_ax], where[b_ax], near(c_ax, -d), 16)))
-        own = cut(rows_at(k, where[a_ax], where[b_ax], None, 64))
-        for d in (2, 1, 3):
-            m2[k, d] = net.send(own, own, dev(b_ax, d))
-
-    over = []
-
-    def to_mate(rows):
-        over.append((net.send(cut(rows), cut(rows), net.mate()), rows))
-
-    for k in range(3):
-        a_ax, b_ax, c_ax = orders[k]
-        for d in (1, 3, 2):
-            net.recv(m2[k, d], cut(rows_at(k, where[a_ax], near(b_ax, -d), None, 64)))
-        rows = rows_at(k, where[a_ax])
-        for d in DIRS:
-            m3[k, d] = net.send(cut(rows), cut(rows), dev(a_ax, d))
-        to_mate(rows)
-    for k in range(3):
-        for d in DIRS:
-            net.recv(m3[k, d], cut(rows_at(k, near(orders[k][0], -d))))
-            rows = part_at(k, -d, side[d])
-            m4[k, d] = net.send(cut(rows), cut(rows), dev(orders[k][0], d))
-        for d in DIRS:
-            to_mate(rows_at(k, near(orders[k][0], -d)))
-    for k in range(3):
-        for d in DIRS:
-            rows = part_at(k, 2, side[d])
-            net.recv(m4[k, d], cut(rows))
-            to_mate(rows)
+    each(gather1, *lead)
+    each(gather2, *early)
+    each(gather1, *tail)
+    each(gather2, *lead)
+    each(gather3, *early)
+    each(gather2, *tail)
+    each(gather3, *lead)
+    each(gather4, *early)
+    each(gather3, *tail)
+    each(gather4, *lead)
+    each(gather5, *early)
+    each(gather4, *tail)
+    each(gather5, *lead)
+    each(gather5, *tail)
     net.recv(tot_mate, s2.at[1 - c])
     totals = s2[0] + s2[1]
     loss_ref[0] = jnp.sum(totals[0:8]) * (1.0 / (PAIRS * NROW * NCOL))
     dscale_ref[0] = jnp.sum(totals[8:16])
-    for number, rows in over:
-        net.recv(number, out.at[rows, give])
+    for number, ch, rows in over:
+        net.recv(number, at_mate(ch, rows))
     net.finish()
 
 
@@ -692,8 +754,8 @@
             vmem((3, 16, HALF), BF16),
             vmem((3, 4, 16, 128), F32),
             vmem((2, 16, 128), F32),
-            pltpu.SemaphoreType.DMA((256,)),
-            pltpu.SemaphoreType.DMA((256,)),
+            pltpu.SemaphoreType.DMA((288,)),
+            pltpu.SemaphoreType.DMA((288,)),
             pltpu.SemaphoreType.DMA((8,)),
         ],
         compiler_params=pltpu.CompilerParams(
@@ -703,8 +765,8 @@
             flops=19 * 10**9, bytes_accessed=24 * 10**6, transcendentals=8 * 10**6
         ),
     )(
-        jnp.exp(log_scale), image_pooled, text_pooled, image_proj, text_proj,
-        pair_index.astype(F32).reshape(1, PAIRS),
+        log_scale, image_pooled, text_pooled, image_proj, text_proj,
+        pair_index.reshape(1, PAIRS),
     )
     dwt = weights[:DT].astype(F32)
     dwi = weights[DT : DT + DI].astype(F32)

time: 162 us -> 165 us (1.019)
  Pallas kernels: 145 us -> 149 us
    pallas_call x1, Pallas kernels: 145 us -> 149 us  [local(): pl.pallas_call(kernel, name='contrastive_loss', out_shape=(jax.ShapeDtype...]
where the time goes in v3:
time: 165 us
  Pallas kernels  149 us (90%)
  other arithmetic  9.6 us (6%)
  between operations  4.74 us (3%)
  local copies, waits for them, and re-layouts  1.75 us (1%)
    pallas_call x1, Pallas kernels, local(): pl.pallas_call(kernel, name='contrastive_loss', out_shape=(jax.ShapeDtype...  149 us
    convert_element_type x1, other arithmetic, local(): dwt = weights[:DT].astype(F32)  5.51 us
    convert_element_type x1, other arithmetic, local(): dwi = weights[DT:DT + DI].astype(F32)  4.09 us

profile of v3, /device:TPU:1, one launch (start us, length us, event | category | flops | bytes accessed | tf_op | source)
XLA Modules:
  0.0 164.7 jit_solution(2681098896602619498)
XLA Ops:
  1.3 148.6 %contrastive_loss.1 = (bf16[3072,1280]{1,0:T(8,128)(2,1)}, bf16[128,1664]{1,0:T(8,128)(2,1)}, bf16[128,1280]{1,0:T(8,128)(2,1)}, f32[1]{0:T(128)}, f32[1]{0:T(128)}) custom-call(f32[1]{0:T(128)S(6)} %copy.16.scale_ref, bf16[128,1664]{1,0:T(8,128)(2,1)} %pi.1, bf16[128,1280]{1,0:T(8,128)(2,1)} %pt.1, bf16[1664,1280]{1,0:T(8,128)(2,1)} %wi_hbm.1, ...), custom_call_target="tpu_custom_call" | custom-call | flops 19000000512 | bytes 24000000 | tf_op jit(solution)/shard_map/contrastive_loss/pallas_call | solution.py:699
  149.9 0.0 copy-start
  149.9 5.5 %slice_convert_fusion.1 = f32[1280,1280]{1,0:T(8,128)} fusion(bf16[3072,1280]{1,0:T(8,128)(2,1)} %get-tuple-element.14), kind=kLoop, calls=%fused_computation.1 | loop fusion | flops 1638400 | bytes 9830400 | tf_op jit(solution)/shard_map/convert_element_type | solution.py:771
  155.5 0.3 copy-done
  155.7 0.0 copy-start.1
  155.7 0.0 copy-start.2
  155.7 4.1 %slice_convert_fusion = f32[1664,1280]{1,0:T(8,128)} fusion(bf16[3072,1280]{1,0:T(8,128)(2,1)S(1)} %copy-done), kind=kLoop, calls=%fused_computation | loop fusion | flops 2129920 | bytes 12779520 | tf_op jit(solution)/shard_map/convert_element_type | solution.py:772
  160.4 0.0 copy-done.1
  160.4 0.8 copy.18
  161.2 0.0 copy-done.2
  161.2 0.7 copy.19
Async XLA Ops:
  149.9 5.8 %copy-start = (bf16[3072,1280]{1,0:T(8,128)(2,1)S(1)}, bf16[3072,1280]{1,0:T(8,128)(2,1)}, u32[]{:S(2)}) copy-start(bf16[3072,1280]{1,0:T(8,128)(2,1)} %get-tuple-element.14) | copy-start | bytes 23592964
  155.7 4.7 %copy-start.1 = (bf16[128,1664]{1,0:T(8,128)(2,1)S(1)}, bf16[128,1664]{1,0:T(8,128)(2,1)}, u32[]{:S(2)}) copy-start(bf16[128,1664]{1,0:T(8,128)(2,1)} %get-tuple-element.23) | copy-start | bytes 1277956
  155.7 5.5 %copy-start.2 = (bf16[128,1280]{1,0:T(8,128)(2,1)S(1)}, bf16[128,1280]{1,0:T(8,128)(2,1)}, u32[]{:S(2)}) copy-start(bf16[128,1280]{1,0:T(8,128)(2,1)} %get-tuple-element.24) | copy-start | bytes 983044

commit v4 on v3

--- a/solution.py
+++ b/solution.py
@@ -30,7 +30,7 @@
         self.x, self.c = row // 2, row % 2
         self.y, self.z = col // 4, col % 4
         self.count = 0
-        self.started = []
+        self.started = {}
 
     def dev(self, dx=0, dy=0, dz=0):
         return (
@@ -69,14 +69,18 @@
         self.count += 1
         copy = self.copy(number, src, dst, device)
         copy.start()
-        self.started.append(copy)
+        self.started[number] = copy
         return number
 
     def recv(self, number, dst):
         self.copy(number, dst, dst, self.mate()).wait_recv()
 
+    def drain(self, numbers):
+        for number in numbers:
+            self.started.pop(number).wait_send()
+
     def finish(self):
-        for copy in self.started:
+        for copy in self.started.values():
             copy.wait_send()
 
 
@@ -174,15 +178,16 @@
         for d in DIRS:
             part = half(img, me_col, h)
             f1[h, d] = net.send(part, part, fdev(h, d))
-    for h in (0, 1):
-        for d in DIRS:
-            part = half(img, me_col, h)
-            g1[h, d] = net.send(part, part, gdev(h, d))
     load_t.wait()
     txt[tblock(0, c), :] = embed(pt, wt, unit_t, norm_t)
     for d in DIRS:
         part = txt.at[tblock(0, c)]
         x1[d] = net.send(part, part, net.dev(dx=d))
+    net.drain(f1.values())
+    for h in (0, 1):
+        for d in DIRS:
+            part = half(img, me_col, h)
+            g1[h, d] = net.send(part, part, gdev(h, d))
 
     def to_mate(dx):
         part = txt.at[tblock(dx, c)]
@@ -317,9 +322,8 @@
     first = (me_col * NROW * PAIRS).astype(F32)
     place = lax.broadcasted_iota(jnp.int32, (PAIRS, PAIRS), 1).astype(F32) + first
 
-    def grad(qa, qb):
-        rows = []
-        for q in (qa, qb):
+    def soft_grad(*pair_of):
+        for q in pair_of:
             lrow = sublanes(rowl[pl.ds(q, 1), :])
             target = sublanes(pid[q][0:1, :]) - place
             hit_sum = jnp.zeros((PAIRS, PAIRS), F32)
@@ -336,10 +340,16 @@
                 gb[here, at] = g.astype(BF16)
             acc[0] += hit_sum
             acc[1] += dot_sum
-            rows.append(gb[here, :])
+
+    def image_product(qa, qb):
+        rows = [gb[pl.ds(pl.multiple_of(q * PAIRS, PAIRS), PAIRS), :] for q in (qa, qb)]
         prod = jnp.dot(jnp.concatenate(rows, axis=0), txt[...], preferred_element_type=F32)
         pimg[qa] = prod[:PAIRS].astype(BF16)
         pimg[qb] = prod[PAIRS:].astype(BF16)
+
+    def grad(qa, qb):
+        soft_grad(qa, qb)
+        image_product(qa, qb)
 
     rg1n, rg2n, rf1n, rf2n = {}, {}, {}, {}
     slot = {2: 0, 1: 1, -1: 2, 0: 3}
@@ -385,11 +395,9 @@
     in_pairs(grad, ((0, 2), (1, 1)))
     scatter1(1, 0)
     scatter2(2)
-    in_pairs(grad, ((1, -1), (-1, 1)), ((-1, -1), (1, 0)))
-    scatter2(1)
-    scatter2(-1)
-    in_pairs(grad, ((0, 1), (-1, 0)), ((0, -1), (0, 0)))
-    scatter2(0)
+    near_pairs = (((1, -1), (-1, 1)), ((-1, -1), (1, 0)))
+    last_pairs = (((0, 1), (-1, 0)), ((0, -1), (0, 0)))
+    in_pairs(soft_grad, *near_pairs, *last_pairs)
 
     mate_n, tx1n, tx2n = {}, {}, {}
 
@@ -409,22 +417,28 @@
         return ptxt[tblock(dx, c), :].astype(F32) + rc[xx].astype(F32)
 
     text_product(2)
-    text_product(1)
-    for h in (0, 1):
-        rb[h, 0] = line_sum(h, 2).astype(BF16)
-        for d in DIRS:
-            at = pl.ds(0 if d == 1 else 32, 32)
-            rf1n[h, d] = net.send(rb.at[h, 0, at], rf1.at[h, side[d]], fdev(h, d))
+    in_pairs(image_product, *near_pairs)
+    scatter2(1)
+    scatter2(-1)
     ptxt[tblock(2, c), :] = text_pair(2).astype(BF16)
     for d in DIRS:
         tx1n[d] = net.send(ptxt.at[tsub(2, c, d)], rx1.at[side[d]], net.dev(dx=d))
+    text_product(1)
     text_product(-1)
+    for h in (0, 1):
+        rb[h, 0] = line_sum(h, 2).astype(BF16)
+        for d in DIRS:
+            at = pl.ds(0 if d == 1 else 32, 32)
+            rf1n[h, d] = net.send(rb.at[h, 0, at], rf1.at[h, side[d]], fdev(h, d))
+    in_pairs(image_product, *last_pairs)
     for d in DIRS:
         ptxt[tblock(d, c), :] = text_pair(d).astype(BF16)
         net.recv(tx1n[d], rx1.at[side[d]])
         part = ptxt.at[tsub(d, c, d)]
         part[...] = (part[...].astype(F32) + rx1[side[d]].astype(F32)).astype(BF16)
         tx2n[d] = net.send(ptxt.at[tblock(d, c)], rx2.at[side[d]], net.dev(dx=d))
+    net.drain(rg2n[h, j, d] for h in (0, 1) for j in (1, -1) for d in DIRS)
+    scatter2(0)
     text_product(0)
     for h in (0, 1):
         for d in DIRS:
@@ -522,14 +536,15 @@
     def to_mate_w(ch, rows):
         over.append((net.send(cut(ch, rows), cut(ch, rows), net.mate()), ch, rows))
 
-    def reduce1(ch):
+    def reduce1(ch, behind=()):
         k, lane = ch[0], pl.ds(ch[1], ch[2])
+        net.drain(behind)
         for d in DIRS:
             n1[ch, d] = net.send(
                 w.at[part_at(k, 2, side[d]), lane], r1.at[k, side[d], :, lane], step(k, d)
             )
 
-    def reduce2(ch):
+    def reduce2(ch, behind=()):
         k, lane = ch[0], pl.ds(ch[1], ch[2])
         for d in DIRS:
             net.recv(n1[ch, d], r1.at[k, side[d], :, lane])
@@ -537,12 +552,14 @@
             w[got, lane] = (w[got, lane].astype(F32) + r1[k, side[d], :, lane].astype(F32)).astype(
                 BF16
             )
+        net.drain(behind)
+        for d in DIRS:
             n2[ch, d] = net.send(
                 w.at[rows_at(k, near(orders[k][0], d)), lane], r2.at[k, side[d], :, lane],
                 step(k, d),
             )
 
-    def reduce3(ch):
+    def reduce3(ch, behind=()):
         k, lane = ch[0], pl.ds(ch[1], ch[2])
         a_ax, b_ax, _ = orders[k]
         total = w[rows_at(k, where[a_ax]), lane].astype(F32)
@@ -550,11 +567,12 @@
             net.recv(n2[ch, d], r2.at[k, side[d], :, lane])
             total += r2[k, side[d], :, lane].astype(F32)
         q1[k, :, lane] = total.astype(BF16)
+        net.drain(behind)
         for d in (2, 1, 3):
             to = pl.ds(pl.multiple_of(64 * near(b_ax, d), 64), 64)
             n3[ch, d] = net.send(q1.at[k, to, lane], r3.at[k, d - 1, :, lane], dev(b_ax, d))
 
-    def reduce4(ch):
+    def reduce4(ch, behind=()):
         k, lane = ch[0], pl.ds(ch[1], ch[2])
         _, b_ax, c_ax = orders[k]
         total = q1[k, pl.ds(pl.multiple_of(64 * where[b_ax], 64), 64), lane].astype(F32)
@@ -562,11 +580,12 @@
             net.recv(n3[ch, d], r3.at[k, d - 1, :, lane])
             total += r3[k, d - 1, :, lane].astype(F32)
         q2[k, :, lane] = total.astype(BF16)
+        net.drain(behind)
         for d in (2, 1, 3):
             to = pl.ds(pl.multiple_of(16 * near(c_ax, d), 16), 16)
             n4[ch, d] = net.send(q2.at[k, to, lane], r4.at[k, d - 1, :, lane], dev(c_ax, d))
 
-    def gather1(ch):
+    def gather1(ch, behind=()):
         k, lane = ch[0], pl.ds(ch[1], ch[2])
         a_ax, b_ax, c_ax = orders[k]
         total = q2[k, pl.ds(pl.multiple_of(16 * where[c_ax], 16), 16), lane].astype(F32)
@@ -575,12 +594,13 @@
             total += r4[k, d - 1, :, lane].astype(F32)
         fin[k, :, lane] = total.astype(BF16)
         own = cut(ch, rows_at(k, where[a_ax], where[b_ax], where[c_ax], 16))
+        net.drain(behind)
         for d in (2, 1, 3):
             m1[ch, d] = net.send(fin.at[k, :, lane], own, dev(c_ax, d))
         back[ch] = pltpu.make_async_copy(fin.at[k, :, lane], own, local_sem.at[2 + len(back)])
         back[ch].start()
 
-    def gather2(ch):
+    def gather2(ch, behind=()):
         k = ch[0]
         a_ax, b_ax, c_ax = orders[k]
         back[ch].wait()
@@ -588,23 +608,27 @@
             rows = rows_at(k, where[a_ax], where[b_ax], near(c_ax, -d), 16)
             net.recv(m1[ch, d], cut(ch, rows))
         own = cut(ch, rows_at(k, where[a_ax], where[b_ax], None, 64))
+        net.drain(behind)
         for d in (2, 1, 3):
             m2[ch, d] = net.send(own, own, dev(b_ax, d))
 
-    def gather3(ch):
+    def gather3(ch, behind=()):
         k = ch[0]
         a_ax, b_ax, _ = orders[k]
         for d in (1, 3, 2):
             net.recv(m2[ch, d], cut(ch, rows_at(k, where[a_ax], near(b_ax, -d), None, 64)))
         rows = rows_at(k, where[a_ax])
+        net.drain(behind)
         for d in DIRS:
             m3[ch, d] = net.send(cut(ch, rows), cut(ch, rows), step(k, d))
         to_mate_w(ch, rows)
 
-    def gather4(ch):
+    def gather4(ch, behind=()):
         k = ch[0]
         for d in DIRS:
             net.recv(m3[ch, d], cut(ch, rows_at(k, near(orders[k][0], -d))))
+        net.drain(behind)
+        for d in DIRS:
             rows = cut(ch, part_at(k, -d, side[d]))
             m4[ch, d] = net.send(rows, rows, step(k, d))
         for d in DIRS:
@@ -616,17 +640,14 @@
             net.recv(m4[ch, d], cut(ch, rows))
             to_mate_w(ch, rows)
 
-    def each(work, *chunks):
-        for ch in chunks:
+    def both(work, sent, ways):
+        for ch in wide:
             work(ch)
-
-    early = (wide[0], slim[0])
-    lead = (wide[1], wide[2])
-    tail = (slim[1], slim[2])
+        for ch, first in zip(slim, wide):
+            work(ch, [sent[first, d] for d in ways])
 
     net.recv(dt_n, dt.at[other])
     weights(0, DT, dt)
-    each(reduce1, *early)
 
     halves = []
     for h in (0, 1):
@@ -636,11 +657,9 @@
             total += rf2[h, side[d]].astype(F32)
         halves.append(scale * total)
     di_n = normal_grad(jnp.concatenate(halves, axis=0), unit_i, norm_i, dz_i, di)
-    each(reduce2, *early)
     net.recv(di_n, di.at[other])
     weights(DT, DI, di)
-    each(reduce1, *lead)
-    each(reduce1, *tail)
+    both(reduce1, n1, DIRS)
 
     def pooled_grad(dz, proj, result, rows):
         @pl.loop(0, rows // 128)
@@ -650,37 +669,24 @@
                 dz[...], proj[at, :], (((1,), (1,)), ((), ())), preferred_element_type=F32
             ).astype(BF16)
 
-    pooled_grad(dz_i, wi, dpi, DI)
-    each(reduce2, *lead)
-    each(reduce3, *early)
-    each(reduce2, *tail)
+    both(reduce2, n2, DIRS)
     s4[1, y] = tot_recv(0)
     tot_send(1)
+    pooled_grad(dz_i, wi, dpi, DI)
     pooled_grad(dz_t, wt, dpt, DT)
-    each(reduce3, *lead)
-    each(reduce4, *early)
-    each(reduce3, *tail)
+    hops = (1, 2, 3)
+    both(reduce3, n3, hops)
     s4[2, z] = tot_recv(1)
     tot_send(2)
-    each(reduce4, *lead)
-    each(gather1, *early)
-    each(reduce4, *tail)
+    both(reduce4, n4, hops)
     s2[c] = tot_recv(2)
     tot_mate = net.send(s2.at[c], s2.at[c], net.mate())
-    each(gather1, *lead)
-    each(gather2, *early)
-    each(gather1, *tail)
-    each(gather2, *lead)
-    each(gather3, *early)
-    each(gather2, *tail)
-    each(gather3, *lead)
-    each(gather4, *early)
-    each(gather3, *tail)
-    each(gather4, *lead)
-    each(gather5, *early)
-    each(gather4, *tail)
-    each(gather5, *lead)
-    each(gather5, *tail)
+    both(gather1, m1, hops)
+    both(gather2, m2, hops)
+    both(gather3, m3, DIRS)
+    both(gather4, m4, DIRS)
+    for ch in wide + slim:
+        gather5(ch)
     net.recv(tot_mate, s2.at[1 - c])
     totals = s2[0] + s2[1]
     loss_ref[0] = jnp.sum(totals[0:8]) * (1.0 / (PAIRS * NROW * NCOL))

time: 165 us -> 156 us (0.945)
  Pallas kernels: 149 us -> 139 us
    pallas_call x1, Pallas kernels: 149 us -> 139 us  [local(): pl.pallas_call(kernel, name='contrastive_loss', out_shape=(jax.ShapeDtype...]
where the time goes in v4:
time: 156 us; the launch traced here: 155 us
  Pallas kernels  139 us (89%)
  other arithmetic  9.6 us (6%)
  between operations  4.74 us (3%)
  local copies, waits for them, and re-layouts  1.75 us (1%)
    pallas_call x1, Pallas kernels, local(): pl.pallas_call(kernel, name='contrastive_loss', out_shape=(jax.ShapeDtype...  139 us
    convert_element_type x1, other arithmetic, local(): dwt = weights[:DT].astype(F32)  5.51 us
    convert_element_type x1, other arithmetic, local(): dwi = weights[DT:DT + DI].astype(F32)  4.09 us

profile of v4, /device:TPU:1, one launch (start us, length us, event | category | flops | bytes accessed | tf_op | source)
XLA Modules:
  0.0 155.4 jit_solution(6467723236507858920)
XLA Ops:
  1.3 139.3 %contrastive_loss.1 = (bf16[3072,1280]{1,0:T(8,128)(2,1)}, bf16[128,1664]{1,0:T(8,128)(2,1)}, bf16[128,1280]{1,0:T(8,128)(2,1)}, f32[1]{0:T(128)}, f32[1]{0:T(128)}) custom-call(f32[1]{0:T(128)S(6)} %copy.16.scale_ref, bf16[128,1664]{1,0:T(8,128)(2,1)} %pi.1, bf16[128,1280]{1,0:T(8,128)(2,1)} %pt.1, bf16[1664,1280]{1,0:T(8,128)(2,1)} %wi_hbm.1, ...), custom_call_target="tpu_custom_call" | custom-call | flops 19000000512 | bytes 24000000 | tf_op jit(solution)/shard_map/contrastive_loss/pallas_call | solution.py:705
  140.6 0.0 copy-start
  140.6 5.5 %slice_convert_fusion.1 = f32[1280,1280]{1,0:T(8,128)} fusion(bf16[3072,1280]{1,0:T(8,128)(2,1)} %get-tuple-element.14), kind=kLoop, calls=%fused_computation.1 | loop fusion | flops 1638400 | bytes 9830400 | tf_op jit(solution)/shard_map/convert_element_type | solution.py:777
  146.1 0.3 copy-done
  146.4 0.0 copy-start.1
  146.4 0.0 copy-start.2
  146.4 4.1 %slice_convert_fusion = f32[1664,1280]{1,0:T(8,128)} fusion(bf16[3072,1280]{1,0:T(8,128)(2,1)S(1)} %copy-done), kind=kLoop, calls=%fused_computation | loop fusion | flops 2129920 | bytes 12779520 | tf_op jit(solution)/shard_map/convert_element_type | solution.py:778
  151.1 0.0 copy-done.1
  151.1 0.8 copy.18
  151.9 0.0 copy-done.2
  151.9 0.7 copy.19
Async XLA Ops:
  140.6 5.8 %copy-start = (bf16[3072,1280]{1,0:T(8,128)(2,1)S(1)}, bf16[3072,1280]{1,0:T(8,128)(2,1)}, u32[]{:S(2)}) copy-start(bf16[3072,1280]{1,0:T(8,128)(2,1)} %get-tuple-element.14) | copy-start | bytes 23592964
  146.4 4.7 %copy-start.1 = (bf16[128,1664]{1,0:T(8,128)(2,1)S(1)}, bf16[128,1664]{1,0:T(8,128)(2,1)}, u32[]{:S(2)}) copy-start(bf16[128,1664]{1,0:T(8,128)(2,1)} %get-tuple-element.23) | copy-start | bytes 1277956
  146.4 5.5 %copy-start.2 = (bf16[128,1280]{1,0:T(8,128)(2,1)S(1)}, bf16[128,1280]{1,0:T(8,128)(2,1)}, u32[]{:S(2)}) copy-start(bf16[128,1280]{1,0:T(8,128)(2,1)} %get-tuple-element.24) | copy-start | bytes 983044

commit v5 on v4

--- a/solution.py
+++ b/solution.py
@@ -21,6 +21,9 @@
 DIRS = (1, -1)
 STEPS = (2, 1, -1, 0)
 WROWS = DI + DT + 128
+LANES = ((0, 256), (256, 256), (512, 128))
+HOLD = False
+CAST = 128
 
 
 class Net:
@@ -511,13 +514,22 @@
         return pl.ds(pl.multiple_of(1024 * k + 256 * near(orders[k][0], d) + 128 * s, 128), 128)
 
     def weights(first_row, rows, right):
+        tall = rows // 4
+
+        @pl.loop(0, 4)
+        def _(i):
+            at = pl.ds(pl.multiple_of(first_row + i * tall, 16), tall)
+            w[at, :] = jnp.dot(turned[at, :], right[...], preferred_element_type=F32).astype(BF16)
+
+    def pooled_grad(dz, proj, result, rows):
         @pl.loop(0, rows // 128)
         def _(i):
-            at = pl.ds(pl.multiple_of(first_row + i * 128, 128), 128)
-            w[at, :] = jnp.dot(turned[at, :], right[...], preferred_element_type=F32).astype(BF16)
-
-    wide = [(k, 0, 384) for k in range(3)]
-    slim = [(k, 384, 256) for k in range(3)]
+            at = pl.ds(pl.multiple_of(i * 128, 128), 128)
+            result[:, at] = lax.dot_general(
+                dz[...], proj[at, :], (((1,), (1,)), ((), ())), preferred_element_type=F32
+            ).astype(BF16)
+
+    groups = [[(k, first, size) for k in range(3)] for first, size in LANES]
     n1, n2, n3, n4 = {}, {}, {}, {}
     m1, m2, m3, m4, back = {}, {}, {}, {}, {}
     over = []
@@ -641,13 +653,14 @@
             to_mate_w(ch, rows)
 
     def both(work, sent, ways):
-        for ch in wide:
-            work(ch)
-        for ch, first in zip(slim, wide):
-            work(ch, [sent[first, d] for d in ways])
+        for n, group in enumerate(groups):
+            for k, ch in enumerate(group):
+                hold = HOLD and n > 0
+                work(ch, [sent[groups[n - 1][k], d] for d in ways] if hold else ())
 
     net.recv(dt_n, dt.at[other])
     weights(0, DT, dt)
+    pooled_grad(dz_t, wt, dpt, DT)
 
     halves = []
     for h in (0, 1):
@@ -660,20 +673,11 @@
     net.recv(di_n, di.at[other])
     weights(DT, DI, di)
     both(reduce1, n1, DIRS)
-
-    def pooled_grad(dz, proj, result, rows):
-        @pl.loop(0, rows // 128)
-        def _(i):
-            at = pl.ds(pl.multiple_of(i * 128, 128), 128)
-            result[:, at] = lax.dot_general(
-                dz[...], proj[at, :], (((1,), (1,)), ((), ())), preferred_element_type=F32
-            ).astype(BF16)
+    pooled_grad(dz_i, wi, dpi, DI)
 
     both(reduce2, n2, DIRS)
     s4[1, y] = tot_recv(0)
     tot_send(1)
-    pooled_grad(dz_i, wi, dpi, DI)
-    pooled_grad(dz_t, wt, dpt, DT)
     hops = (1, 2, 3)
     both(reduce3, n3, hops)
     s4[2, z] = tot_recv(1)
@@ -685,8 +689,9 @@
     both(gather2, m2, hops)
     both(gather3, m3, DIRS)
     both(gather4, m4, DIRS)
-    for ch in wide + slim:
-        gather5(ch)
+    for group in groups:
+        for ch in group:
+            gather5(ch)
     net.recv(tot_mate, s2.at[1 - c])
     totals = s2[0] + s2[1]
     loss_ref[0] = jnp.sum(totals[0:8]) * (1.0 / (PAIRS * NROW * NCOL))
@@ -694,6 +699,28 @@
     for number, ch, rows in over:
         net.recv(number, at_mate(ch, rows))
     net.finish()
+
+
+def cast_kernel(w, dpi, dpt, wt_out, wi_out, dpi_out, dpt_out, narrow, wide, got, put, passed):
+    hand_on = [
+        pltpu.make_async_copy(dpi, dpi_out, passed.at[0]),
+        pltpu.make_async_copy(dpt, dpt_out, passed.at[1]),
+    ]
+    blocks = (DT + DI) // CAST
+    reads, writes = [], []
+    for i in range(blocks):
+        reads.append(pltpu.make_async_copy(w.at[pl.ds(i * CAST, CAST)], narrow.at[i], got.at[i]))
+        first = i * CAST
+        to = wt_out.at[pl.ds(first, CAST)] if first < DT else wi_out.at[pl.ds(first - DT, CAST)]
+        writes.append(pltpu.make_async_copy(wide.at[i], to, put.at[i]))
+    for copy in reads + hand_on:
+        copy.start()
+    for i in range(blocks):
+        reads[i].wait()
+        wide[i] = narrow[i].astype(F32)
+        writes[i].start()
+    for copy in writes + hand_on:
+        copy.wait()
 
 
 def local(image_pooled, text_pooled, image_proj, text_proj, log_scale, pair_index):
@@ -760,9 +787,9 @@
             vmem((3, 16, HALF), BF16),
             vmem((3, 4, 16, 128), F32),
             vmem((2, 16, 128), F32),
-            pltpu.SemaphoreType.DMA((288,)),
-            pltpu.SemaphoreType.DMA((288,)),
-            pltpu.SemaphoreType.DMA((8,)),
+            pltpu.SemaphoreType.DMA((384,)),
+            pltpu.SemaphoreType.DMA((384,)),
+            pltpu.SemaphoreType.DMA((16,)),
         ],
         compiler_params=pltpu.CompilerParams(
             collective_id=0, has_side_effects=True, vmem_limit_bytes=60 * 1024 * 1024
@@ -774,8 +801,28 @@
         log_scale, image_pooled, text_pooled, image_proj, text_proj,
         pair_index.reshape(1, PAIRS),
     )
-    dwt = weights[:DT].astype(F32)
-    dwi = weights[DT : DT + DI].astype(F32)
+    blocks = (DT + DI) // CAST
+    dwt, dwi, dpi, dpt = pl.pallas_call(
+        cast_kernel,
+        name="casts",
+        out_shape=(
+            jax.ShapeDtypeStruct((DT, EMB), F32),
+            jax.ShapeDtypeStruct((DI, EMB), F32),
+            jax.ShapeDtypeStruct((PAIRS, DI), BF16),
+            jax.ShapeDtypeStruct((PAIRS, DT), BF16),
+        ),
+        in_specs=[far, held, held],
+        out_specs=(far, far, far, far),
+        scratch_shapes=[
+            vmem((blocks, CAST, EMB), BF16),
+            vmem((blocks, CAST, EMB), F32),
+            pltpu.SemaphoreType.DMA((blocks,)),
+            pltpu.SemaphoreType.DMA((blocks,)),
+            pltpu.SemaphoreType.DMA((2,)),
+        ],
+        compiler_params=pltpu.CompilerParams(vmem_limit_bytes=48 * 1024 * 1024),
+        cost_estimate=pl.CostEstimate(flops=0, bytes_accessed=24 * 10**6, transcendentals=0),
+    )(weights, dpi, dpt)
     return (loss, dpi, dpt, dwi, dwt, dscale)
 
 

time: 156 us -> 149 us (0.955)
  other arithmetic: 9.6 us -> 0 us
  Pallas kernels: 139 us -> 142 us
    convert_element_type x2 -> x0, other arithmetic: 9.6 us -> none  [the longest x1 5.51 us: local(): dwt = weights[:DT].astype(F32)]
    pallas_call x0 -> x1, Pallas kernels: none -> 7.89 us  [local(): pl.pallas_call(cast_kernel, name='casts', out_shape=(jax.ShapeDtypeStruct...]
    pallas_call x1, Pallas kernels: 139 us -> 134 us  [local(): pl.pallas_call(kernel, name='contrastive_loss', out_shape=(jax.ShapeDtype...]
where the time goes in v5:
time: 149 us
  Pallas kernels  142 us (95%)
  between operations  4.72 us (3%)
  local copies, waits for them, and re-layouts  1.97 us (1%)
    pallas_call x1, Pallas kernels, local(): pl.pallas_call(kernel, name='contrastive_loss', out_shape=(jax.ShapeDtype...  134 us
    pallas_call x1, Pallas kernels, local(): pl.pallas_call(cast_kernel, name='casts', out_shape=(jax.ShapeDtypeStruct...  7.89 us

profile of v5, /device:TPU:1, one launch (start us, length us, event | category | flops | bytes accessed | tf_op | source)
XLA Modules:
  0.0 148.8 jit_solution(1694995286390905445)
XLA Ops:
  1.3 134.3 %contrastive_loss.1 = (bf16[3072,1280]{1,0:T(8,128)(2,1)}, bf16[128,1664]{1,0:T(8,128)(2,1)}, bf16[128,1280]{1,0:T(8,128)(2,1)}, f32[1]{0:T(128)}, f32[1]{0:T(128)}) custom-call(f32[1]{0:T(128)S(6)} %copy.14.scale_ref, bf16[128,1664]{1,0:T(8,128)(2,1)} %pi.1, bf16[128,1280]{1,0:T(8,128)(2,1)} %pt.1, bf16[1664,1280]{1,0:T(8,128)(2,1)} %wi_hbm.1, ...), custom_call_target="tpu_custom_call" | custom-call | flops 19000000512 | bytes 24000000 | tf_op jit(solution)/shard_map/contrastive_loss/pallas_call | solution.py:732
  135.6 0.0 copy-start
  135.6 1.0 copy-done
  136.6 0.0 copy-start.1
  136.6 1.0 copy-done.1
  137.5 7.9 %casts.1 = (f32[1280,1280]{1,0:T(8,128)}, f32[1664,1280]{1,0:T(8,128)}, bf16[128,1664]{1,0:T(8,128)(2,1)}, bf16[128,1280]{1,0:T(8,128)(2,1)}) custom-call(bf16[3072,1280]{1,0:T(8,128)(2,1)} %get-tuple-element.16.w, bf16[128,1664]{1,0:T(8,128)(2,1)S(1)} %copy-done, bf16[128,1280]{1,0:T(8,128)(2,1)S(1)} %copy-done.1), custom_call_target="tpu_custom_call" | custom-call | bytes 24000000 | tf_op jit(solution)/shard_map/casts/pallas_call | solution.py:805
Async XLA Ops:
  135.6 1.0 copy-start
  136.6 1.0 copy-start.1

commit v6 on v5

--- a/solution.py
+++ b/solution.py
@@ -35,9 +35,10 @@
         self.count = 0
         self.started = {}
 
-    def dev(self, dx=0, dy=0, dz=0):
+    def dev(self, dx=0, dy=0, dz=0, swap=0):
+        core = 1 - self.c if swap else self.c
         return (
-            2 * ((self.x + dx + 4) % 4) + self.c,
+            2 * ((self.x + dx + 4) % 4) + core,
             4 * ((self.y + dy + 4) % 4) + (self.z + dz + 4) % 4,
         )
 
@@ -45,9 +46,8 @@
         return (2 * self.x + 1 - self.c, 4 * self.y + self.z)
 
     def greet(self):
-        others = [self.mate()]
-        for d in (1, 2, 3):
-            others += [self.dev(dx=d), self.dev(dy=d), self.dev(dz=d)]
+        others = [self.dev(dx=d, swap=s) for d in range(4) for s in (0, 1)][1:]
+        others += [self.dev(dy=d, dz=e) for d in range(4) for e in range(4)][1:]
         self.others = len(others)
         for other in others:
             pl.semaphore_signal(
@@ -111,7 +111,7 @@
     scale_ref, pi, pt, wi_hbm, wt_hbm, pair, out, dpi, dpt, loss_ref, dscale_ref,
     img, txt, pid, scores, gb, pimg, ptxt,
     rg1, rg2, rb, rf1, rf2, rc, rx1, rx2,
-    cmax, csum, rowl, rowz, rowy, coll, colx, colc, acc,
+    cmax, csum, rowl, rowq, coll, colq, acc,
     wi, wt, unit_i, unit_t, norm_i, norm_t, turned, dz_i, dz_t, di, dt,
     w, r1, r2, q1, r3, q2, r4, fin, s4, s2,
     send_sem, recv_sem, local_sem,
@@ -293,34 +293,30 @@
     last_hop(2)
     in_pairs(score, ((-1, 2), (2, 2)))
 
-    rz, ry, lx = {}, {}, {}
-    rowz[z] = rowl[...]
-    for d in (1, 2, 3):
-        rz[d] = net.send(rowz.at[z], rowz.at[z], net.dev(dz=d))
+    rows_n, cols_n = {}, {}
+    plane = [(dy, dz) for dy in (0, 1, 3, 2) for dz in (0, 1, 3, 2)][1:]
+    line = [(dx, swap) for dx in (0, 1, 3, 2) for swap in (0, 1)][1:]
+    rowq[me_col] = rowl[...]
+    for dy, dz in plane:
+        own = rowq.at[me_col]
+        rows_n[dy, dz] = net.send(own, own, net.dev(dy=dy, dz=dz))
     peak = jnp.max(cmax[...], axis=0, keepdims=True)
     lcol = peak + jnp.log(jnp.sum(csum[...] * jnp.exp(cmax[...] - peak), axis=0, keepdims=True))
+    me_row = 2 * x + c
     for r in range(NROW):
-        coll[r : r + 1, :] = lcol[:, r * PAIRS : (r + 1) * PAIRS]
-    colx[x] = coll[...]
+        colq[me_row, r : r + 1, :] = lcol[:, r * PAIRS : (r + 1) * PAIRS]
+    for dx, swap in line:
+        own = colq.at[me_row]
+        cols_n[dx, swap] = net.send(own, own, net.dev(dx=dx, swap=swap))
     for d in (1, 2, 3):
-        lx[d] = net.send(colx.at[x], colx.at[x], net.dev(dx=d))
-    for d in (1, 2, 3):
-        net.recv(rz[d], rowz.at[(z - d + 4) % 4])
-    rowy[y] = lse_over([rowz[i] for i in range(4)])
-    for d in (1, 2, 3):
-        ry[d] = net.send(rowy.at[y], rowy.at[y], net.dev(dy=d))
-    for d in (1, 2, 3):
-        net.recv(lx[d], colx.at[(x - d + 4) % 4])
-    colc[c] = lse_over([colx[i] for i in range(4)])
-    lc = net.send(colc.at[c], colc.at[c], net.mate())
-    for d in (1, 2, 3):
-        line = pid.at[pl.ds(4 * ((y - d + 4) % 4), 4)]
-        net.recv(py[d], line)
-    for d in (1, 2, 3):
-        net.recv(ry[d], rowy.at[(y - d + 4) % 4])
-    rowl[...] = lse_over([rowy[i] for i in range(4)])
-    net.recv(lc, colc.at[1 - c])
-    coll[...] = lse_over([colc[i] for i in range(2)])
+        net.recv(py[d], pid.at[pl.ds(4 * ((y - d + 4) % 4), 4)])
+    for dy, dz in plane:
+        net.recv(rows_n[dy, dz], rowq.at[rel(-dy, -dz)])
+    rowl[...] = lse_over([rowq[i] for i in range(NCOL)])
+    for dx, swap in line:
+        flip = c + swap - 2 * c * swap
+        net.recv(cols_n[dx, swap], colq.at[2 * ((x - dx + 4) % 4) + flip])
+    coll[...] = lse_over([colq[i] for i in range(NROW)])
 
     first = (me_col * NROW * PAIRS).astype(F32)
     place = lax.broadcasted_iota(jnp.int32, (PAIRS, PAIRS), 1).astype(F32) + first
@@ -760,11 +756,9 @@
             vmem((8, cols), F32),
             vmem((8, cols), F32),
             vmem((NCOL, PAIRS), F32),
-            vmem((4, NCOL, PAIRS), F32),
-            vmem((4, NCOL, PAIRS), F32),
+            vmem((NCOL, NCOL, PAIRS), F32),
             vmem((NROW, PAIRS), F32),
-            vmem((4, NROW, PAIRS), F32),
-            vmem((2, NROW, PAIRS), F32),
+            vmem((NROW, NROW, PAIRS), F32),
             vmem((2, PAIRS, PAIRS), F32),
             vmem((DI, EMB), BF16),
             vmem((DT, EMB), BF16),

time: 149 us -> 149 us (level)
  no operation moved by 1% of the time
where the time goes in v6:
time: 149 us; the launch traced here: 148 us
  Pallas kernels  142 us (95%)
  between operations  4.72 us (3%)
  local copies, waits for them, and re-layouts  1.97 us (1%)
    pallas_call x1, Pallas kernels, local(): pl.pallas_call(kernel, name='contrastive_loss', out_shape=(jax.ShapeDtype...  134 us
    pallas_call x1, Pallas kernels, local(): pl.pallas_call(cast_kernel, name='casts', out_shape=(jax.ShapeDtypeStruct...  7.89 us

profile of v6, /device:TPU:1, one launch (start us, length us, event | category | flops | bytes accessed | tf_op | source)
XLA Modules:
  0.0 148.5 jit_solution(13550086959864047765)
XLA Ops:
  1.3 133.9 %contrastive_loss.1 = (bf16[3072,1280]{1,0:T(8,128)(2,1)}, bf16[128,1664]{1,0:T(8,128)(2,1)}, bf16[128,1280]{1,0:T(8,128)(2,1)}, f32[1]{0:T(128)}, f32[1]{0:T(128)}) custom-call(f32[1]{0:T(128)S(6)} %copy.14.scale_ref, bf16[128,1664]{1,0:T(8,128)(2,1)} %pi.1, bf16[128,1280]{1,0:T(8,128)(2,1)} %pt.1, bf16[1664,1280]{1,0:T(8,128)(2,1)} %wi_hbm.1, ...), custom_call_target="tpu_custom_call" | custom-call | flops 19000000512 | bytes 24000000 | tf_op jit(solution)/shard_map/contrastive_loss/pallas_call | solution.py:728
  135.2 0.0 copy-start
  135.2 1.0 copy-done
  136.2 0.0 copy-start.1
  136.2 1.0 copy-done.1
  137.2 7.9 %casts.1 = (f32[1280,1280]{1,0:T(8,128)}, f32[1664,1280]{1,0:T(8,128)}, bf16[128,1664]{1,0:T(8,128)(2,1)}, bf16[128,1280]{1,0:T(8,128)(2,1)}) custom-call(bf16[3072,1280]{1,0:T(8,128)(2,1)} %get-tuple-element.16.w, bf16[128,1664]{1,0:T(8,128)(2,1)S(1)} %copy-done, bf16[128,1280]{1,0:T(8,128)(2,1)S(1)} %copy-done.1), custom_call_target="tpu_custom_call" | custom-call | bytes 24000000 | tf_op jit(solution)/shard_map/casts/pallas_call | solution.py:799
Async XLA Ops:
  135.2 1.0 copy-start
  136.2 1.0 copy-start.1
